TPU v7x, 256 devices: a whole 4x4x8 slice. The times are simulated.
256 devices in a mesh: sec: 64 (over z_lo, x, y, core), tp: 4 (over z_hi).
Axes of the slice: x: 4, y: 4, z: 8 (z_hi: 4, z_lo: 2; z = z_hi * 2 + z_lo), core: 2. Of those that a mesh axis runs over, the one named last changes fastest.
Arguments:
- pixels: bfloat16 [12288, 3072], P('sec'), may hold values from -6 to 6
- w_encode: bfloat16 [3072, 2048], P(None, 'tp'), may hold values from -0.109375 to 0.109375
- w_latent: bfloat16 [2048, 64], P('tp'), may hold values from -0.25 to 0.25
- source_row: int32 [12288], P('sec'), may hold values from 0 to 12287, each once
- w_embed: bfloat16 [64, 3072], replicated, may hold values from -0.75 to 0.75
- mod_shift: float32 [3072], replicated, may hold values from -3 to 3
- mod_scale: float32 [3072], replicated, may hold values from 0.1 to 1.9
- gate: float32 [3072], replicated, may hold values from 0.1 to 1.9
- q_gain: float32 [128], replicated, may hold values from 1.5 to 3
- k_gain: float32 [128], replicated, may hold values from 1.5 to 3
- w_qkv: bfloat16 [3, 3072, 1536], P(None, 'sec', 'tp'), may hold values from -0.109375 to 0.109375
- w_out: bfloat16 [1536, 3072], P('tp', 'sec'), may hold values from -0.15625 to 0.15625
Outputs:
- latents: bfloat16 [12288, 64], P('sec')
- block_out: bfloat16 [12288, 3072], P('sec', 'tp')
Inputs may be any that keep to these rules, and one draw needn't show every extreme that they name: `source_row`: each latent row appears exactly once.
All inputs are finite; a program needn't handle non-finite values.
Results may differ from a plain program's by a relative error of at most 0.04.
Values may be sent and summed in bfloat16 or wider, within the bound.
A program may use at most 128 MiB of HBM per device.

v0:
```python
import jax
import jax.numpy as jnp
from jax import lax
from jax.sharding import PartitionSpec as P

HD = 128


def head_norm(values, heads, width, gains):
    shaped = values.reshape(values.shape[0], heads, width)
    return shaped * lax.rsqrt(jnp.mean(shaped * shaped, axis=2, keepdims=True) + 1e-06) * gains


def block_count(count, rows):
    shards = count // rows
    limit = max(1, 2048 // rows)
    best = 1
    for cand in range(1, shards + 1):
        if shards % cand == 0 and cand <= limit:
            best = cand
    return shards // best


def per_device(
    pixels,
    w_encode,
    w_latent,
    source_row,
    w_embed,
    mod_shift,
    mod_scale,
    gate,
    q_gain,
    k_gain,
    w_qkv,
    w_out,
):
    rows = pixels.shape[0]
    width = HD
    heads = w_qkv.shape[2] // width
    hidden = jax.nn.silu(jnp.dot(pixels, w_encode, preferred_element_type=jnp.float32)).astype(
        jnp.bfloat16
    )
    partial_lat = jnp.dot(hidden, w_latent, preferred_element_type=jnp.float32)
    encoded = lax.psum(partial_lat.astype(jnp.bfloat16), "tp")
    every_row = lax.all_gather(encoded, "sec", axis=0, tiled=True)
    latents = every_row[source_row]
    embedded = jnp.dot(latents, w_embed, preferred_element_type=jnp.float32)
    center = embedded - jnp.mean(embedded, axis=1, keepdims=True)
    normed = center * lax.rsqrt(jnp.mean(center * center, axis=1, keepdims=True) + 1e-06)
    modulated = (normed * mod_scale + mod_shift).astype(jnp.bfloat16)
    projections = jnp.einsum(
        "td,cdh->cth",
        modulated,
        lax.all_gather(w_qkv, "sec", axis=1, tiled=True),
        preferred_element_type=jnp.float32,
    )
    query = head_norm(projections[0], heads, width, q_gain).astype(jnp.bfloat16)
    keyrow = (
        head_norm(projections[1], heads, width, k_gain)
        .astype(jnp.bfloat16)
        .reshape(rows, heads * width)
    )
    valrow = projections[2].astype(jnp.bfloat16)
    factor = 1.0 / jnp.sqrt(jnp.float32(width))

    def attend_block(carry, block):
        running, totals, accum = carry
        keys_blk, vals_blk = block
        keys_in = keys_blk.reshape(keys_blk.shape[0], heads, width)
        vals_in = vals_blk.reshape(vals_blk.shape[0], heads, width)
        scores = (
            jnp.einsum("thd,nhd->htn", query, keys_in, preferred_element_type=jnp.float32) * factor
        )
        newmax = jnp.maximum(running, jnp.max(scores, axis=2))
        shrink = jnp.exp(running - newmax)
        expos = jnp.exp(scores - newmax[:, :, None])
        totals = totals * shrink + jnp.sum(expos, axis=2)
        added = jnp.einsum(
            "htn,nhd->thd", expos.astype(jnp.bfloat16), vals_in, preferred_element_type=jnp.float32
        )
        accum = accum * shrink.T[:, :, None] + added
        return ((newmax, totals, accum), None)

    start_carry = (
        jnp.full((heads, rows), -1e30, jnp.float32),
        jnp.zeros((heads, rows), jnp.float32),
        jnp.zeros((rows, heads, width), jnp.float32),
    )
    carry = start_carry
    pieces = (
        lax.all_gather(keyrow, "sec", axis=0, tiled=True),
        lax.all_gather(valrow, "sec", axis=0, tiled=True),
    )
    count = pieces[0].shape[0]
    blocks = block_count(count, rows)
    size = count // blocks
    keys_all = pieces[0].reshape(blocks, size, pieces[0].shape[1])
    vals_all = pieces[1].reshape(blocks, size, pieces[1].shape[1])
    carry, unused = lax.scan(attend_block, carry, (keys_all, vals_all))
    running, totals, accum = carry
    attended = (accum / totals.T[:, :, None]).astype(jnp.bfloat16).reshape(rows, heads * width)
    terms = jnp.dot(
        attended,
        lax.all_gather(w_out, "sec", axis=1, tiled=True),
        preferred_element_type=jnp.float32,
    )
    projected = lax.psum_scatter(
        terms.astype(jnp.bfloat16), "tp", scatter_dimension=1, tiled=True
    ).astype(jnp.float32)
    quarter = projected.shape[1]
    offset = lax.axis_index("tp") * quarter
    embed_part = lax.dynamic_slice_in_dim(embedded, offset, quarter, 1)
    gate_part = lax.dynamic_slice_in_dim(gate, offset, quarter, 0)
    block_out = (embed_part + gate_part * projected).astype(jnp.bfloat16)
    return (latents, block_out)


def solution(mesh):
    placed = (
        P("sec", None),
        P(None, "tp"),
        P("tp", None),
        P("sec"),
        P(),
        P(),
        P(),
        P(),
        P(),
        P(),
        P(None, "sec", "tp"),
        P("tp", "sec"),
    )
    return jax.shard_map(
        per_device,
        mesh=mesh,
        in_specs=placed,
        out_specs=(P("sec", None), P("sec", "tp")),
        check_vma=False,
    )
```

profile of v0, /device:TPU:1, one launch (start us, length us, event | category | flops | bytes accessed | tf_op | source)
XLA Modules:
  0.0 670.5 jit_solution(3119605997822803500)
XLA Ops:
  11.3 20.1 %psum.7 = bf16[192,64]{0,1:T(8,128)(2,1)} all-reduce(bf16[192,64]{0,1:T(8,128)(2,1)S(1)} %convolution_convert_fusion.1), channel_id=1, replica_groups=mesh['sec'=64,'tp'=4] {'tp'}, use_global_device_ids=true, to_apply=%region_0.1 | all-reduce | flops 12288 | bytes 49152 | tf_op jit(solution)/shard_map/psum | solution.py:45
  32.3 107.4 %all-gather.16.cloned.1.call-done = bf16[64,192,64]{1,2,0:T(8,128)(2,1)} async-done(((bf16[1,192,64]{1,2,0:T(8,128)(2,1)}), bf16[64,192,64]{1,2,0:T(8,128)(2,1)}) %all-gather.16.cloned.1.call-update) | async-done | bytes 1572880 | tf_op jit(solution)/shard_map/all_gather | solution.py:46
  139.6 4.5 copy.61
  144.1 3.0 gather_fusion
  150.5 102.0 %all-gather.8.cloned.1.call-done = bf16[3,3072,384]{2,1,0:T(8,128)(2,1)} async-done(((bf16[3,48,384]{2,1,0:T(8,128)(2,1)}), bf16[3,3072,384]{2,1,0:T(8,128)(2,1)}) %all-gather.8.cloned.1.call-update) | async-done | bytes 7077904 | tf_op jit(solution)/shard_map/all_gather | solution.py:55
  252.5 5.5 convolution_bitcast_fusion
  271.5 107.2 %all-gather.10.cloned.1.call-done = bf16[12288,384]{1,0:T(8,128)(2,1)} async-done(((bf16[192,384]{1,0:T(8,128)(2,1)}), bf16[12288,384]{1,0:T(8,128)(2,1)}) %all-gather.10.cloned.1.call-update) | async-done | bytes 9437200 | tf_op jit(solution)/shard_map/all_gather | solution.py:92
  378.7 116.4 %all-gather.14.cloned.1.call-done = bf16[1,12288,384]{2,1,0:T(8,128)(2,1)} async-done(((bf16[1,192,384]{2,1,0:T(8,128)(2,1)}), bf16[1,12288,384]{2,1,0:T(8,128)(2,1)}) %all-gather.14.cloned.1.call-update) | async-done | bytes 9437200 | tf_op jit(solution)/shard_map/all_gather | solution.py:93
  495.1 128.2 %while.15 = (s32[]{:T(128)}, f32[3,192]{1,0:T(4,128)S(1)}, f32[3,192]{1,0:T(4,128)S(1)}, f32[192,3,128]{2,0,1:T(8,128)S(1)}, bf16[8,1536,384]{2,1,0:T(8,128)(2,1...) while((s32[]{:T(128)}, f32[3,192]{1,0:T(4,128)S(1)}, ...), condition=%wide.region_8.9_spmd.clone, body=%wide.region_5.8_spmd.clone.sunk | while | flops 458517888 | bytes 37343368 | solution.py:100
  495.1 3.2 constant_dynamic-slice_fusion.3
  498.3 2.4 copy.76
  500.8 3.8 bitcast_reduce_fusion.2
  504.6 2.4 copy.77
  507.0 3.2 fusion.57
  511.1 3.3 constant_dynamic-slice_fusion.3
  514.3 2.4 copy.76
  516.8 3.8 bitcast_reduce_fusion.2
  520.6 2.4 copy.77
  523.0 3.3 fusion.57
  527.1 3.3 constant_dynamic-slice_fusion.3
  530.4 2.4 copy.76
  532.8 3.8 bitcast_reduce_fusion.2
  536.6 2.4 copy.77
  539.0 3.2 fusion.57
  543.2 3.3 constant_dynamic-slice_fusion.3
  546.4 2.4 copy.76
  548.8 3.8 bitcast_reduce_fusion.2
  552.7 2.4 copy.77
  555.1 3.2 fusion.57
  559.2 3.3 constant_dynamic-slice_fusion.3
  562.5 2.4 copy.76
  564.9 3.8 bitcast_reduce_fusion.2
  568.7 2.4 copy.77
  571.1 3.2 fusion.57
  575.3 3.3 constant_dynamic-slice_fusion.3
  580.9 3.8 bitcast_reduce_fusion.2
  584.8 2.4 copy.77
  587.2 3.2 fusion.57
  591.3 3.3 constant_dynamic-slice_fusion.3
  596.9 3.8 bitcast_reduce_fusion.2
  600.8 2.4 copy.77
  603.2 3.2 fusion.57
  607.3 3.3 constant_dynamic-slice_fusion.3
  612.9 3.8 bitcast_reduce_fusion.2
  616.7 2.4 copy.77
  619.2 3.2 fusion.57
  623.3 3.7 convolution_convert_fusion
  628.5 33.1 %reduce-scatter.2.cloned.1.call-done = bf16[192,768]{1,0:T(8,128)(2,1)} async-done(((bf16[192,3072]{1,0:T(8,128)(2,1)}), bf16[192,768]{1,0:T(8,128)(2,1)}) %reduce-scatter.2.cloned.1.call-update) | async-done | bytes 294928 | tf_op jit(solution)/shard_map/reduce_scatter | solution.py:108
  (110 shorter events, 39.2 us)
Async XLA Ops:
  7.2 1.9 copy-start
  7.2 25.0 %copy-start.6 = (s32[192]{0:T(256)S(1)}, s32[192]{0:T(256)}, u32[]{:S(2)}) copy-start(s32[192]{0:T(256)} %param.17) | copy-start | bytes 2308
  7.2 25.1 %copy-start.8 = (f32[128]{0:T(128)S(1)}, f32[128]{0:T(128)}, u32[]{:S(2)}) copy-start(f32[128]{0:T(128)} %param.23) | copy-start | bytes 1540
  7.2 132.4 %all-gather.16.cloned.1.call-start = ((), (), s32[]{:S(2)}) async-start(), calls=%async_computation.6 | async-start | bytes 2129920 | tf_op jit(solution)/shard_map/all_gather | solution.py:46
  31.4 221.0 %all-gather.8.cloned.1.call-start = ((), (), s32[]{:S(2)}) async-start(), calls=%async_computation.1 | async-start | bytes 7188480 | tf_op jit(solution)/shard_map/all_gather | solution.py:55
  32.2 346.5 %all-gather.10.cloned.1.call-start = ((), (), s32[]{:S(2)}) async-start(), calls=%async_computation.2 | async-start | bytes 9584640 | tf_op jit(solution)/shard_map/all_gather | solution.py:92
  147.1 3.4 copy-start.4
  147.1 105.4 %copy-start.9 = (f32[3072]{0:T(1024)S(1)}, f32[3072]{0:T(1024)}, u32[]{:S(2)}) copy-start(f32[3072]{0:T(1024)} %param.19) | copy-start | bytes 36868
  147.1 105.4 %copy-start.10 = (f32[3072]{0:T(1024)S(1)}, f32[3072]{0:T(1024)}, u32[]{:S(2)}) copy-start(f32[3072]{0:T(1024)} %param.20) | copy-start | bytes 36868
  148.7 1.4 copy-start.2
  258.0 1.2 copy-start.3
  259.1 10.4 %copy-start.7 = (f32[128]{0:T(128)S(1)}, f32[128]{0:T(128)}, u32[]{:S(2)}) copy-start(f32[128]{0:T(128)} %param.22) | copy-start | bytes 1540
  264.0 231.1 %all-gather.14.cloned.1.call-start = ((), (), s32[]{:S(2)}) async-start(), calls=%async_computation.5 | async-start | bytes 9584640 | tf_op jit(solution)/shard_map/all_gather | solution.py:93
  265.7 357.6 %all-gather.12.cloned.1.call-start = ((), (), s32[]{:S(2)}) async-start(), calls=%async_computation.3 | async-start | bytes 2396160 | tf_op jit(solution)/shard_map/all_gather | solution.py:105
  266.3 395.4 %reduce-scatter.2.cloned.1.call-start = ((), (), s32[]{:S(2)}) async-start(), calls=%async_computation.4 | async-start | bytes 1474560 | tf_op jit(solution)/shard_map/reduce_scatter | solution.py:108
  507.0 3.4 copy-start.1
  523.0 3.4 copy-start.1
  539.0 3.4 copy-start.1
  555.1 3.4 copy-start.1
  571.1 3.4 copy-start.1
  587.2 3.4 copy-start.1
  603.2 3.4 copy-start.1
  619.2 3.4 copy-start.1
  623.3 4.5 copy-start.5
Sparse Core Ops, SparseCore 0:
  31.5 108.0 all-gather.15
  141.4 110.9 all-gather.7
  264.1 114.5 all-gather.9
  380.4 114.6 all-gather.13
  496.8 105.4 all-gather.11
  627.2 34.4 reduce-scatter.1
where the time goes:
time: 672 us; the launch traced here: 670 us
  waiting for transfers between devices  467 us (69%)
  local copies, waits for them, and re-layouts  84.1 us (13%)
  matrix products  69.3 us (10%)
  blocking collectives  20.1 us (3%)
  other arithmetic  14.7 us (2%)
  between operations  14.3 us (2%)
    all_gather x1, waiting for transfers between devices, per_device(): lax.all_gather(valrow, 'sec', axis=0, tiled=True)  116 us
    all_gather x1, waiting for transfers between devices, per_device(): every_row = lax.all_gather(encoded, 'sec', axis=0, tiled=True)  107 us
    all_gather x1, waiting for transfers between devices, per_device(): lax.all_gather(keyrow, 'sec', axis=0, tiled=True)  107 us
    all_gather x1, waiting for transfers between devices, per_device(): lax.all_gather(w_qkv, 'sec', axis=1, tiled=True)  102 us
    dynamic_slice x24, local copies, waits for them, and re-layouts, per_device(): carry, unused = lax.scan(attend_block, carry, (keys_all, vals_all))  64.7 us
    reduce_scatter x1, waiting for transfers between devices, per_device(): lax.psum_scatter(terms.astype(jnp.bfloat16), 'tp', scatter_dimension=1, t...  33.1 us
    dot_general x8, matrix products, attend_block(): jnp.einsum('thd,nhd->htn', query, keys_in, preferred_element_type=jnp.flo...  30.4 us
    dot_general x8, matrix products, attend_block(): jnp.einsum('htn,nhd->thd', expos.astype(jnp.bfloat16), vals_in, preferred...  25.9 us
  transfers between devices with their start and end apart: 6, of which 5 were waited for; matrix products, arithmetic and copies ran while one was open for 21% of the time, Pallas kernels for 0%

commit v1 on v0

v1 whole, which is shorter than its diff:
```python
import functools

import jax
import jax.numpy as jnp
from jax import lax
from jax.experimental import pallas as pl
from jax.experimental.pallas import tpu as pltpu
from jax.sharding import PartitionSpec as P

MESH = pl.DeviceIdType.MESH
HD = 128
HEADS = 3
LAT = 64
ROWS = 192
LANES = 256
WID = HEADS * HD
F32 = jnp.float32
BF16 = jnp.bfloat16
NT = (((1,), (1,)), ((), ()))
NN = (((1,), (0,)), ((), ()))
TN = (((0,), (0,)), ((), ()))
PIECE = 128
STAT = 64
MROW = 80
EPS = 1e-6
TOP = 100.0
LOG2E = 1.4426950408889634
VMEM_LIMIT = 48 * 1024 * 1024


def dot(a, b, dims):
    return lax.dot_general(a, b, dims, preferred_element_type=F32)


def split(value):
    high = value.astype(BF16).astype(F32)
    return high, value - high


def barrier_with(greet, waits):
    barrier = pltpu.get_barrier_semaphore()
    for device in greet:
        pl.semaphore_signal(barrier, inc=1, device_id=device, device_id_type=MESH)
    pl.semaphore_wait(barrier, waits)


def remote(src, dst, send, recv, device):
    return pltpu.make_async_remote_copy(
        src_ref=src, dst_ref=dst, send_sem=send, recv_sem=recv, device_id=device, device_id_type=MESH
    )


def reduce_kernel(lat_ref, wp_ref, lat_out, w_out, lat_in, core_in, half, x_in, y_in, total, send, recv):
    s = lax.axis_index("sec")
    t = lax.axis_index("tp")
    z = s // 32
    x = (s // 8) % 4
    y = (s // 2) % 4
    c = s % 2
    sibling = {"sec": s + 1 - 2 * c}
    tp_peers = [{"tp": (t + k) % 4} for k in range(1, 4)]
    x_at = [(x + k) % 4 for k in range(1, 4)]
    x_peers = [{"sec": s + (xx - x) * 8} for xx in x_at]
    b = z * 4 + y
    b_at = [(b + k) % 8 for k in range(1, 8)]
    b_peers = [{"sec": (bb // 4) * 32 + x * 8 + (bb % 4) * 2 + c} for bb in b_at]
    everyone = tp_peers + [sibling] + x_peers + b_peers
    barrier_with(everyone, len(everyone))

    tp_copies = []
    for k in range(3):
        copy = remote(lat_ref, lat_in.at[t], send.at[k], recv.at[k], tp_peers[k])
        copy.start()
        tp_copies.append(copy)
    other = pl.multiple_of((1 - c) * 576, 576)
    mine = pl.multiple_of(c * 576, 576)
    core_copy = remote(wp_ref.at[pl.ds(other, 576)], core_in, send.at[3], recv.at[3], sibling)
    core_copy.start()
    lat_in[t] = lat_ref[...]
    core_copy.wait_recv()
    half[...] = (wp_ref[pl.ds(mine, 576), :].astype(F32) + core_in[...].astype(F32)).astype(BF16)
    x_copies = []
    for k in range(3):
        rows = pl.ds(pl.multiple_of(x_at[k] * 144, 144), 144)
        copy = remote(half.at[rows], x_in.at[x], send.at[4 + k], recv.at[4 + k], x_peers[k])
        copy.start()
        x_copies.append(copy)
    x_in[x] = half[pl.ds(pl.multiple_of(x * 144, 144), 144), :]
    for copy in x_copies:
        copy.wait_recv()
    added = x_in[0].astype(F32)
    for k in range(1, 4):
        added += x_in[k].astype(F32)
    y_in[b] = added.astype(BF16)
    b_copies = []
    for k in range(7):
        copy = remote(y_in.at[b], y_in.at[b], send.at[7 + k], recv.at[7 + k], b_peers[k])
        copy.start()
        b_copies.append(copy)
    for copy in tp_copies:
        copy.wait_recv()
    summed = lat_in[0].astype(F32)
    for k in range(1, 4):
        summed += lat_in[k].astype(F32)
    lat_out[...] = summed.astype(BF16)
    for copy in b_copies:
        copy.wait_recv()
    added = y_in[0].astype(F32)
    for k in range(1, 8):
        added += y_in[k].astype(F32)
    place = pl.ds(pl.multiple_of(c * 576 + x * 144, 144), 144)
    total[place, :] = added.astype(BF16)
    g_copies = []
    for k in range(3):
        copy = remote(total.at[place], total.at[place], send.at[14 + k], recv.at[14 + k], x_peers[k])
        copy.start()
        g_copies.append(copy)
    for copy in g_copies:
        copy.wait_recv()
    last = remote(total.at[pl.ds(mine, 576)], total.at[pl.ds(mine, 576)], send.at[17], recv.at[17], sibling)
    last.start()
    last.wait_recv()
    w_out[...] = total[...]
    for copy in tp_copies + [core_copy] + x_copies + b_copies + g_copies + [last]:
        copy.wait_send()


def reduce_call(lat_part, w_part):
    whole = pl.BlockSpec(memory_space=pltpu.VMEM)
    return pl.pallas_call(
        reduce_kernel,
        out_shape=(
            jax.ShapeDtypeStruct((LAT, LANES), BF16),
            jax.ShapeDtypeStruct((3 * WID, HD), BF16),
        ),
        in_specs=[whole] * 2,
        out_specs=(whole, whole),
        scratch_shapes=[
            pltpu.VMEM((4, LAT, LANES), BF16),
            pltpu.VMEM((576, HD), BF16),
            pltpu.VMEM((576, HD), BF16),
            pltpu.VMEM((4, 144, HD), BF16),
            pltpu.VMEM((8, 144, HD), BF16),
            pltpu.VMEM((1152, HD), BF16),
            pltpu.SemaphoreType.DMA((18,)),
            pltpu.SemaphoreType.DMA((18,)),
        ],
        compiler_params=pltpu.CompilerParams(collective_id=0, has_side_effects=True, vmem_limit_bytes=VMEM_LIMIT),
    )(lat_part, w_part)


def owner_kernel(lat_ref, w_ref, embed_ref, wo_ref, piece_ref, m_ref):
    lat = lat_ref[...]
    embedded = dot(embed_ref[...], lat, TN)
    center = embedded - jnp.mean(embedded, axis=0, keepdims=True)
    rstd = lax.rsqrt(jnp.mean(center * center, axis=0, keepdims=True) + EPS)
    piece_ref[0:LAT, :] = lat
    stats = [rstd]
    keys = w_ref[WID : 2 * WID, :]
    raw = dot(keys[:, 0:LAT], lat, NN) * rstd + keys[:, LAT : LAT + 1].astype(F32)
    for h in range(HEADS):
        part = raw[h * HD : (h + 1) * HD, :]
        stats.append(lax.rsqrt(jnp.mean(part * part, axis=0, keepdims=True) + EPS))
    row = lax.broadcasted_iota(jnp.int32, (16, LANES), 0)
    block = jnp.zeros((16, LANES), F32)
    for i, value in enumerate(stats):
        high, low = split(value)
        block = jnp.where(row == 2 * i, high, block)
        block = jnp.where(row == 2 * i + 1, low, block)
    piece_ref[STAT : STAT + 16, :] = block.astype(BF16)
    lane = lax.broadcasted_iota(jnp.int32, (48, HD), 1)
    terms = [
        dot(wo_ref[h * HD : (h + 1) * HD, :], w_ref[2 * WID + h * HD : 2 * WID + (h + 1) * HD, :], TN)
        for h in range(HEADS)
    ]
    first = jnp.where(lane < LAT, terms[0], pltpu.roll(terms[1], LAT, 1))
    second = jnp.where(lane < LAT, terms[2], terms[0] + terms[1] + terms[2])
    m_ref[:, 0:HD] = first.astype(BF16)
    m_ref[:, HD:LANES] = second.astype(BF16)


def owner_call(lat, weights, w_embed, w_out):
    return pl.pallas_call(
        owner_kernel,
        out_shape=(jax.ShapeDtypeStruct((MROW, LANES), BF16), jax.ShapeDtypeStruct((48, LANES), BF16)),
        compiler_params=pltpu.CompilerParams(vmem_limit_bytes=VMEM_LIMIT),
    )(lat, weights, w_embed, w_out)


def gather_kernel(piece_ref, m_ref, slots, own, send, recv, local_sem):
    s = lax.axis_index("sec")
    t = lax.axis_index("tp")
    z = s // 32
    x = (s // 8) % 4
    y = (s // 2) % 4
    c = s % 2
    u = x + c * (y - x)
    v = y + c * (x - y)
    u_stride = 8 - 6 * c
    v_stride = 2 + 6 * c
    sibling = {"sec": s + 1 - 2 * c}
    z_peer = {"sec": s + (1 - 2 * z) * 32}
    u_peers = [{"sec": s + ((u + k) % 4 - u) * u_stride} for k in range(1, 4)]
    v_peers = [{"sec": s + ((v + k) % 4 - v) * v_stride} for k in range(1, 4)]
    m_to = {"tp": s // 16, "sec": ((s % 16) * 4 + t + 1) % 64}
    back = (s + 63) % 64
    m_from = {"tp": back % 4, "sec": t * 16 + back // 4}
    around = [sibling, z_peer] + u_peers + v_peers
    barrier_with(around + [m_from], len(around) + 1)

    move = remote(m_ref, own.at[pl.ds(MROW, 48)], send.at[0], recv.at[0], m_to)
    move.start()
    own[0:MROW, :] = piece_ref[...]
    move.wait_recv()
    at = (v * 4 + u) * 2 + z
    keep = pltpu.make_async_copy(own, slots.at[c, at], local_sem)
    keep.start()
    z_copy = remote(own, slots.at[c, at], send.at[1], recv.at[1], z_peer)
    z_copy.start()
    keep.wait()
    z_copy.wait_recv()
    copies = [move, z_copy]
    pair = pl.ds((v * 4 + u) * 2, 2)
    u_copies = []
    for k in range(3):
        copy = remote(slots.at[c, pair], slots.at[c, pair], send.at[2 + k], recv.at[2 + k], u_peers[k])
        copy.start()
        u_copies.append(copy)
    for copy in u_copies:
        copy.wait_recv()
    group = pl.ds(v * 8, 8)
    v_copies = []
    for k in range(3):
        copy = remote(slots.at[c, group], slots.at[c, group], send.at[5 + k], recv.at[5 + k], v_peers[k])
        copy.start()
        v_copies.append(copy)
    cross = remote(slots.at[c, group], slots.at[c, group], send.at[8], recv.at[8], sibling)
    cross.start()
    crossing = [cross]
    for k in range(3):
        v_copies[k].wait_recv()
        came = pl.ds(((v + 3 - k) % 4) * 8, 8)
        cross = remote(slots.at[c, came], slots.at[c, came], send.at[9 + k], recv.at[9 + k], sibling)
        cross.start()
        crossing.append(cross)
    for copy in crossing:
        copy.wait_recv()
    for copy in copies + u_copies + v_copies + crossing:
        copy.wait_send()


def gather_call(piece, m_part):
    whole = pl.BlockSpec(memory_space=pltpu.VMEM)
    return pl.pallas_call(
        gather_kernel,
        out_shape=jax.ShapeDtypeStruct((2, 32, PIECE, LANES), BF16),
        in_specs=[whole] * 2,
        out_specs=pl.BlockSpec(memory_space=pl.ANY),
        scratch_shapes=[
            pltpu.VMEM((PIECE, LANES), BF16),
            pltpu.SemaphoreType.DMA((12,)),
            pltpu.SemaphoreType.DMA((12,)),
            pltpu.SemaphoreType.DMA,
        ],
        compiler_params=pltpu.CompilerParams(collective_id=1, has_side_effects=True, vmem_limit_bytes=VMEM_LIMIT),
    )(piece, m_part)


def merged(slots, at, rows):
    lane = lax.broadcasted_iota(jnp.int32, (rows.size, HD), 1)
    left = slots[0, at, rows, :]
    right = slots[1, at, rows, :]
    middle = jnp.where(lane < LAT, left[:, HD:].astype(F32), right[:, :HD].astype(F32)).astype(BF16)
    return jnp.concatenate([left[:, :HD], middle, right[:, HD:]], axis=1)


def chunk_of(slots, i, rows):
    return jnp.concatenate([merged(slots, 2 * i, rows), merged(slots, 2 * i + 1, rows)], axis=1)


def attend_kernel(
    slots, src_ref, w_ref, embed_ref, qg_ref, kg_ref, lat_ref, mixed_ref, latq, queries, accum, best
):
    chunk = 768
    lat_rows = pl.ds(0, LAT)
    stat_rows = pl.ds(STAT, 16)
    lane = lax.broadcasted_iota(jnp.int32, (1, chunk), 1)
    source = src_ref[...]

    latq[...] = jnp.zeros_like(latq)

    def pick(i, carry):
        v = i // 4
        u = i % 4
        base0 = u * 8 * ROWS + v * 2 * ROWS
        base1 = v * 8 * ROWS + u * 2 * ROWS + ROWS
        upper = lane // 384
        inner = lane - upper * 384
        token = inner + upper * (32 * ROWS) + jnp.where(inner < ROWS, base0, base1 - ROWS)
        hit = jnp.where(source == token, 1.0, 0.0).astype(BF16)
        latq[:, 0:LAT] += dot(hit, chunk_of(slots, i, lat_rows), NT)
        return carry

    lax.fori_loop(0, 16, pick, 0)
    rows = latq[...].astype(BF16)
    lat_ref[...] = rows[:, 0:LAT]
    embedded = dot(rows[:, 0:LAT], embed_ref[...], NN)
    center = embedded - jnp.mean(embedded, axis=1, keepdims=True)
    rstd = lax.rsqrt(jnp.mean(center * center, axis=1, keepdims=True) + EPS)
    unit = jnp.where(lax.broadcasted_iota(jnp.int32, (16, HD), 1) == LAT, 1.0, 0.0).astype(BF16)
    wide = lax.broadcasted_iota(jnp.int32, (ROWS, HD), 1)
    for h in range(HEADS):
        wq = w_ref[h * HD : (h + 1) * HD, :]
        wk = w_ref[WID + h * HD : WID + (h + 1) * HD, :]
        raw = rstd * dot(rows, wq, NT) + dot(unit, wq, NT)[0:1, :]
        q = raw * lax.rsqrt(jnp.mean(raw * raw, axis=1, keepdims=True) + EPS) * qg_ref[...]
        qk = q * kg_ref[...] * (LOG2E / HD**0.5)
        bound = jnp.sqrt(jnp.sum(qk * qk, axis=1, keepdims=True)) * (1.02 * HD**0.5)
        shift = jnp.maximum(bound - TOP, 0.0)
        high, low = split(qk)
        folded = dot(high.astype(BF16), wk, NN) + dot(low.astype(BF16), wk, NN)
        beta_high, beta_low = split(folded[:, LAT : LAT + 1])
        value = jnp.where(wide < LAT, folded, 0.0)
        value = jnp.where((wide == LAT) | (wide == LAT + 1), beta_high, value)
        value = jnp.where(wide == LAT + 2, beta_low, value)
        value = jnp.where(wide == LAT + 3, -shift, value)
        queries[h] = value.astype(BF16)

    index = lax.broadcasted_iota(jnp.int32, (16, chunk), 0)

    def operands(i):
        lat = chunk_of(slots, i, lat_rows).astype(F32)
        stat = chunk_of(slots, i, stat_rows).astype(F32)
        scale = stat[0:1, :] + stat[1:2, :]
        scaled = lat * scale
        ones = jnp.where(index == 0, 1.0, 0.0)
        vals = jnp.concatenate([scaled.astype(BF16), ones.astype(BF16)], axis=0)
        keys = []
        for h in range(HEADS):
            high = stat[2 + 2 * h : 3 + 2 * h, :]
            low = stat[3 + 2 * h : 4 + 2 * h, :]
            tail = jnp.where((index == 0) | (index == 2), high, 0.0)
            tail = jnp.where(index == 1, low, tail)
            tail = jnp.where(index == 3, 1.0, tail)
            keys.append(jnp.concatenate([(scaled * (high + low)).astype(BF16), tail.astype(BF16)], axis=0))
        return keys, vals

    accum[...] = jnp.zeros_like(accum)

    def attend(i, carry):
        keys, vals = operands(i)
        for h in range(HEADS):
            weights = jnp.exp2(dot(queries[h][:, 0:MROW], keys[h], NN)).astype(BF16)
            accum[h, :, 0:MROW] += dot(weights, vals, NT)
        return carry

    lax.fori_loop(0, 16, attend, 0)
    least = jnp.min(accum[:, :, LAT : LAT + 1])

    @pl.when(jnp.logical_not(least > 2.0**-60))
    def _():
        accum[...] = jnp.zeros_like(accum)
        best[...] = jnp.full_like(best, -1e30)

        def exact(i, carry):
            keys, vals = operands(i)
            for h in range(HEADS):
                scores = dot(queries[h][:, 0:MROW], keys[h], NN)
                old = best[h, :, 0:1]
                new = jnp.maximum(old, jnp.max(scores, axis=1, keepdims=True))
                weights = jnp.exp2(scores - new).astype(BF16)
                accum[h, :, 0:MROW] = accum[h, :, 0:MROW] * jnp.exp2(old - new) + dot(weights, vals, NT)
                best[h] = jnp.broadcast_to(new, (ROWS, HD))
            return carry

        lax.fori_loop(0, 16, exact, 0)

    parts = [accum[h] / accum[h, :, LAT : LAT + 1] for h in range(HEADS)]
    first = jnp.where(wide < LAT, parts[0], pltpu.roll(parts[1], LAT, 1))
    second = jnp.where(wide < LAT, parts[2], jnp.where(wide == LAT, 1.0, 0.0))
    mixed_ref[:, 0:HD] = first.astype(BF16)
    mixed_ref[:, HD:LANES] = second.astype(BF16)


def attend_call(slots, source, weights, w_embed, q_gain, k_gain):
    return pl.pallas_call(
        attend_kernel,
        out_shape=(jax.ShapeDtypeStruct((ROWS, LAT), BF16), jax.ShapeDtypeStruct((ROWS, LANES), BF16)),
        scratch_shapes=[
            pltpu.VMEM((ROWS, HD), F32),
            pltpu.VMEM((HEADS, ROWS, HD), BF16),
            pltpu.VMEM((HEADS, ROWS, HD), F32),
            pltpu.VMEM((HEADS, ROWS, HD), F32),
        ],
        compiler_params=pltpu.CompilerParams(vmem_limit_bytes=VMEM_LIMIT),
    )(slots, source, weights, w_embed, q_gain, k_gain)


def heads_kernel(mixed_ref, out_ref, held, send, recv):
    t = lax.axis_index("tp")
    peers = [{"tp": (t + k) % 4} for k in range(1, 4)]
    barrier_with(peers, 3)
    copies = []
    for k in range(3):
        copy = remote(mixed_ref, held.at[t], send.at[k], recv.at[k], peers[k])
        copy.start()
        copies.append(copy)
    held[t] = mixed_ref[...]
    for copy in copies:
        copy.wait_recv()
    out_ref[...] = held[...]
    for copy in copies:
        copy.wait_send()


def heads_call(mixed):
    whole = pl.BlockSpec(memory_space=pltpu.VMEM)
    return pl.pallas_call(
        heads_kernel,
        out_shape=jax.ShapeDtypeStruct((4, ROWS, LANES), BF16),
        in_specs=[whole],
        out_specs=whole,
        scratch_shapes=[
            pltpu.VMEM((4, ROWS, LANES), BF16),
            pltpu.SemaphoreType.DMA((3,)),
            pltpu.SemaphoreType.DMA((3,)),
        ],
        compiler_params=pltpu.CompilerParams(collective_id=2, has_side_effects=True, vmem_limit_bytes=VMEM_LIMIT),
    )(mixed)


def project_kernel(mixed_ref, slots, lat_ref, embed_ref, gate_ref, out_ref, assembled):
    for place in range(64):
        c, rest = place // 32, place % 32
        v, u, z = rest // 8, (rest // 2) % 4, rest % 2
        x, y = (u, v) if c == 0 else (v, u)
        back = (z * 32 + x * 8 + y * 2 + c + 63) % 64
        assembled[back % 4, (back // 4) * 48 : (back // 4) * 48 + 48, :] = slots[c, rest, MROW:PIECE, :]
    total = dot(mixed_ref[0], assembled[0], NT)
    for k in range(1, 4):
        total += dot(mixed_ref[k], assembled[k], NT)
    embedded = dot(lat_ref[...], embed_ref[...], NN)
    out_ref[...] = (embedded + gate_ref[...] * total).astype(BF16)


def project_call(mixed, slots, latents, embed_part, gate_part):
    return pl.pallas_call(
        project_kernel,
        out_shape=jax.ShapeDtypeStruct((ROWS, 768), BF16),
        scratch_shapes=[pltpu.VMEM((4, 768, LANES), BF16)],
        compiler_params=pltpu.CompilerParams(vmem_limit_bytes=VMEM_LIMIT),
    )(mixed, slots, latents, embed_part, gate_part)


def per_device(
    pixels, w_encode, w_latent, source_row, w_embed, mod_shift, mod_scale, gate, q_gain, k_gain, w_qkv, w_out
):
    s = lax.axis_index("sec")
    t = lax.axis_index("tp")
    hidden = jax.nn.silu(jnp.dot(pixels, w_encode, preferred_element_type=F32)).astype(BF16)
    part = lax.dot_general(w_latent, hidden, (((0,), (1,)), ((), ())), preferred_element_type=F32)
    zero = jnp.zeros((LAT, LANES), BF16)
    lat_part = lax.dynamic_update_slice(zero, part.astype(BF16), (0, LAT * (s % 2)))

    wide = w_embed.astype(F32)
    columns = lax.dynamic_slice_in_dim(wide, s * 48, 48, 1) - jnp.mean(wide, axis=1, keepdims=True)
    columns = columns * lax.dynamic_slice_in_dim(mod_scale, s * 48, 48, 0)[None, :]
    shift = lax.dynamic_slice_in_dim(mod_shift, s * 48, 48, 0)[None, :]
    left = jnp.concatenate([columns, shift, jnp.zeros((HD - LAT - 1, 48), F32)], axis=0)
    w_part = jnp.einsum("idc,fd->icf", w_qkv.astype(F32), left, precision=lax.Precision.HIGHEST)
    w_part = w_part.reshape(3 * WID, HD).astype(BF16)

    lat, weights = reduce_call(lat_part, w_part)
    piece, m_part = owner_call(lat, weights, w_embed, w_out)
    slots = gather_call(piece, m_part)
    latents, mixed = attend_call(
        slots, source_row.reshape(ROWS, 1), weights, w_embed, q_gain.reshape(1, HD), k_gain.reshape(1, HD)
    )
    every = heads_call(mixed)
    embed_part = lax.dynamic_slice_in_dim(w_embed, t * 768, 768, 1)
    gate_part = lax.dynamic_slice_in_dim(gate, t * 768, 768, 0).reshape(1, 768)
    return latents, project_call(every, slots, latents, embed_part, gate_part)


def solution(mesh):
    placed = (
        P("sec", None), P(None, "tp"), P("tp", None), P("sec"), P(), P(), P(), P(), P(), P(),
        P(None, "sec", "tp"), P("tp", "sec"),
    )
    return jax.shard_map(
        per_device, mesh=mesh, in_specs=placed, out_specs=(P("sec", None), P("sec", "tp")), check_vma=False
    )
```

time: 672 us -> 141 us (0.21)
  waiting for transfers between devices: 467 us -> 0 us
  Pallas kernels: 0 us -> 102 us
  matrix products: 69.3 us -> 5.09 us
  local copies, waits for them, and re-layouts: 84.1 us -> 29.5 us
  blocking collectives: 20.1 us -> 0 us
  between operations: 14.3 us -> 0.79 us
  other arithmetic: 14.7 us -> 2.41 us
    all_gather x5 -> x0, waiting for transfers between devices: 433 us -> none  [the longest x1 116 us: per_device(): lax.all_gather(valrow, 'sec', axis=0, tiled=True)]
    pallas_call x0 -> x6, Pallas kernels: none -> 102 us  [the longest x1 37.2 us: gather_call(): pl.pallas_call(gather_kernel, out_shape=jax.ShapeDtypeStruct((2, 32, PIEC...]
    dot_general x20 -> x2, matrix products: 69.3 us -> 5.09 us  [the longest x1 2.93 us: per_device(): lax.dot_general(w_latent, hidden, (((0,), (1,)), ((), ())), preferred_ele...]
    dynamic_slice x25 -> x3, local copies, waits for them, and re-layouts: 65.5 us -> 1.56 us  [the longest x1 0.78 us: per_device(): gate_part = lax.dynamic_slice_in_dim(gate, t * 768, 768, 0).reshape(1, 768)]
    reduce_scatter x1 -> x0, waiting for transfers between devices: 33.1 us -> none  [per_device(): lax.psum_scatter(terms.astype(jnp.bfloat16), 'tp', scatter_dimension=1, t...]
    psum x1 -> x0, blocking collectives: 20.1 us -> none  [per_device(): encoded = lax.psum(partial_lat.astype(jnp.bfloat16), 'tp')]
    unnamed x23 -> x49, local copies, waits for them, and re-layouts: 9.27 us -> 21.7 us
    reduce_sum x11 -> x1, other arithmetic: 7.65 us -> 0.42 us  [per_device(): jnp.mean(wide, axis=1, keepdims=True)]
  transfers between devices with their start and end apart: 6 -> 0, of which waited for: 5 -> 0; matrix products, arithmetic and copies ran while one was open for 21% -> 0% of each run, Pallas kernels for 0% -> 0%
where the time goes in v1:
time: 141 us; the launch traced here: 140 us
  Pallas kernels  102 us (72%)
  local copies, waits for them, and re-layouts  29.5 us (21%)
  matrix products  5.09 us (4%)
  other arithmetic  2.41 us (2%)
    pallas_call x1, Pallas kernels, gather_call(): pl.pallas_call(gather_kernel, out_shape=jax.ShapeDtypeStruct((2, 32, PIEC...  37.2 us
    pallas_call x1, Pallas kernels, reduce_call(): pl.pallas_call(reduce_kernel, out_shape=(jax.ShapeDtypeStruct((LAT, LANES...  27.1 us
    unnamed x49, local copies, waits for them, and re-layouts  21.7 us
    pallas_call x1, Pallas kernels, attend_call(): pl.pallas_call(attend_kernel, out_shape=(jax.ShapeDtypeStruct((ROWS, LAT)...  19.7 us
    pallas_call x1, Pallas kernels, heads_call(): pl.pallas_call(heads_kernel, out_shape=jax.ShapeDtypeStruct((4, ROWS, LAN...  14.8 us
    dot_general x1, matrix products, per_device(): lax.dot_general(w_latent, hidden, (((0,), (1,)), ((), ())), preferred_ele...  2.93 us

profile of v1, /device:TPU:1, one launch (start us, length us, event | category | flops | bytes accessed | tf_op | source)
XLA Modules:
  0.0 139.5 jit_solution(8125411303335681768)
XLA Ops:
  0.6 0.0 copy-start
  0.7 1.9 %copy-done = bf16[3072,512]{1,0:T(8,128)(2,1)S(1)} copy-done((bf16[3072,512]{1,0:T(8,128)(2,1)S(1)}, bf16[3072,512]{1,0:T(8,128)(2,1)}, u32[]{:S(2)}) %copy-start) | copy-done | bytes 3145752
  2.5 2.9 %fusion.1 = bf16[64,192]{1,0:T(8,128)(2,1)} fusion(bf16[512,64]{0,1:T(8,128)(2,1)} %param.14, bf16[192,3072]{1,0:T(8,128)(2,1)} %param.12, bf16[3072,512]{1,0:T(8,128)(2,1)S(1)} %copy-done), kind=kOutput, calls=%fused_computation.3 | convolution fusion | flops 617066496 | bytes 4415488 | tf_op jit(solution)/shard_map/dot_general | solution.py:461
  5.5 0.6 broadcast_in_dim.11
  6.1 1.5 %dynamic_update_slice.3.lat_ref = bf16[64,256]{1,0:T(8,128)(2,1)} dynamic-update-slice(bf16[64,256]{1,0:T(8,128)(2,1)} %broadcast_in_dim.11, bf16[64,192]{1,0:T(8,128)(2,1)} %fusion.1, s32[]{:T(128)} %constant.17.clone.1, s32[]{:T(128)S(6)} %select_n.20) | dynamic-update-slice | bytes 49156 | tf_op jit(solution)/shard_map/dynamic_update_slice | solution.py:463
  7.6 0.8 dynamic_slice.16
  8.4 0.0 copy-done.4
  8.4 1.2 copy.19
  9.5 1.3 convert_element_type.23
  10.8 0.1 copy-done.21
  10.9 0.4 convert_reduce_fusion
  11.3 0.7 subtract_multiply_fusion
  12.0 0.8 dynamic-slice_bitcast_fusion
  12.8 0.7 copy.20
  13.5 0.1 pad.2.clone
  13.5 2.2 %fusion = bf16[3,384,128]{1,2,0:T(8,128)(2,1)} fusion(bf16[3,48,384]{2,1,0:T(8,128)(2,1)} %param.22, f32[1,48]{0,1:T(8,128)} %copy.20, f32[64,48]{0,1:T(8,128)} %subtract_multiply_fusion, f32[128]{0:T(128)S(1)} %pad.2.clone), kind=kOutput, calls=%fused_computation.1 | convolution fusion | flops 85094400 | bytes 418496 | tf_op jit(solution)/shard_map/idc,fd->icf/dot_general | solution.py:470
  15.7 1.8 %copy.21 = bf16[3,384,128]{2,1,0:T(8,128)(2,1)} copy(bf16[3,384,128]{1,2,0:T(8,128)(2,1)} %fusion) | data formatting | bytes 589824 | tf_op jit(solution)/shard_map/convert_element_type | solution.py:471
  17.6 1.0 copy-done.7
  18.5 0.8 copy-done.16
  19.3 27.1 %shard_map.131 = (bf16[64,256]{1,0:T(8,128)(2,1)S(1)}, bf16[1152,128]{1,0:T(8,128)(2,1)S(1)}) custom-call(bf16[64,256]{1,0:T(8,128)(2,1)S(1)} %copy-done.16, bf16[1152,128]{1,0:T(8,128)(2,1)S(1)} %bitcast.17), custom_call_target="tpu_custom_call" | custom-call | tf_op jit(solution)/shard_map/pallas_call | solution.py:130
  46.4 0.0 copy-start.8
  46.4 0.7 copy-done.8
  47.1 0.6 copy-done.17
  47.7 1.5 %copy.22.wo_ref = bf16[384,48]{1,0:T(8,128)(2,1)} copy(bf16[384,48]{0,1:T(8,128)(2,1)} %param.23) | data formatting | bytes 73728 | tf_op args[11]
  49.2 1.0 copy-done.9
  50.2 0.9 copy-done.11
  51.1 0.8 copy-done.18
  51.8 1.4 %shard_map.132 = (bf16[80,256]{1,0:T(8,128)(2,1)S(1)}, bf16[48,256]{1,0:T(8,128)(2,1)S(1)}) custom-call(bf16[64,256]{1,0:T(8,128)(2,1)S(1)} %copy-done.18, bf16[1152,128]{1,0:T(8,128)(2,1)S(1)} %copy-done.9, bf16[64,3072]{1,0:T(8,128)(2,1)S(1)} %copy-done.4, bf16[384,48]{1,0:T(8,128)(2,1)S(1)} %copy-done.11), custom_call_target="tpu_custom_call" | custom-call | tf_op jit(solution)/shard_map/pallas_call | solution.py:183
  53.3 0.0 copy-start.22
  53.3 0.0 copy-start.19
  53.3 0.0 copy-start.20
  53.3 37.2 %shard_map.133.slots = bf16[2,32,128,256]{3,2,1,0:T(8,128)(2,1)S(1)} custom-call(bf16[80,256]{1,0:T(8,128)(2,1)S(1)} %get-tuple-element.10.piece_ref, bf16[48,256]{1,0:T(8,128)(2,1)S(1)} %get-tuple-element.11.m_ref), custom_call_target="tpu_custom_call" | custom-call | tf_op jit(solution)/shard_map/pallas_call | solution.py:254
  90.6 1.9 %copy-done.1 = bf16[2,32,128,256]{3,2,1,0:T(8,128)(2,1)} copy-done((bf16[2,32,128,256]{3,2,1,0:T(8,128)(2,1)}, bf16[2,32,128,256]{3,2,1,0:T(8,128)(2,1)S(1)}, u32[]{:S(2)}) %copy-start.1) | copy-done | bytes 4194328
  92.5 0.8 copy.23.src_ref
  93.3 0.0 copy-done.20
  93.3 2.2 %copy-done.2 = bf16[2,32,128,256]{3,2,1,0:T(8,128)(2,1)S(1)} copy-done((bf16[2,32,128,256]{3,2,1,0:T(8,128)(2,1)S(1)}, bf16[2,32,128,256]{3,2,1,0:T(8,128)(2,1)}, u32[]{:S(2)}) %copy-start.2) | copy-done | bytes 4194328
  95.5 1.0 copy-done.10
  96.4 0.9 copy-done.12
  97.3 19.7 %shard_map.134 = (bf16[192,64]{1,0:T(8,128)(2,1)S(1)}, bf16[192,256]{1,0:T(8,128)(2,1)S(1)}) custom-call(bf16[2,32,128,256]{3,2,1,0:T(8,128)(2,1)S(1)} %copy-done.2, s32[192,1]{1,0:T(8,128)S(1)} %copy-done.12, bf16[1152,128]{1,0:T(8,128)(2,1)S(1)} %copy-done.10, bf16[64,3072]{1,0:T(8,128)(2,1)S(1)} %copy-done.4, f32[1,128]{1,0:T(1,128)S(1)} %bitcast.18, ...), custom_call_target="tpu_custom_call" | custom-call | tf_op jit(solution)/shard_map/pallas_call | solution.py:386
  117.0 0.0 copy-start.13
  117.0 14.8 %shard_map.135.mixed_ref = bf16[4,192,256]{2,1,0:T(8,128)(2,1)S(1)} custom-call(bf16[192,256]{1,0:T(8,128)(2,1)S(1)} %get-tuple-element.13.mixed_ref), custom_call_target="tpu_custom_call" | custom-call | tf_op jit(solution)/shard_map/pallas_call | solution.py:418
  131.8 0.7 copy-done.5
  132.6 0.8 dynamic_slice.19
  133.4 2.2 %copy-done.3 = bf16[2,32,128,256]{3,2,1,0:T(8,128)(2,1)S(1)} copy-done((bf16[2,32,128,256]{3,2,1,0:T(8,128)(2,1)S(1)}, bf16[2,32,128,256]{3,2,1,0:T(8,128)(2,1)}, u32[]{:S(2)}) %copy-start.3) | copy-done | bytes 4194328
  135.6 1.0 copy-done.6
  136.6 0.8 copy-done.14
  137.4 1.5 %shard_map.136 = bf16[192,768]{1,0:T(8,128)(2,1)} custom-call(bf16[4,192,256]{2,1,0:T(8,128)(2,1)S(1)} %copy-done.6, bf16[2,32,128,256]{3,2,1,0:T(8,128)(2,1)S(1)} %copy-done.3, bf16[192,64]{1,0:T(8,128)(2,1)S(1)} %copy-done.14, bf16[64,768]{1,0:T(8,128)(2,1)S(1)} %constant_dynamic-slice_fusion.embed_ref, f32[1,768]{1,0:T(1,128)S(1)} %reshape.26.gate_ref), custom_call_target="tpu_custom_call" | custom-call | tf_op jit(solution)/shard_map/pallas_call | solution.py:447
  138.8 0.7 copy.24
  (25 shorter events, 0.1 us)
Async XLA Ops:
  0.6 1.9 %copy-start = (bf16[3072,512]{1,0:T(8,128)(2,1)S(1)}, bf16[3072,512]{1,0:T(8,128)(2,1)}, u32[]{:S(2)}) copy-start(bf16[3072,512]{1,0:T(8,128)(2,1)} %param.13) | copy-start | bytes 9437188
  2.5 5.8 %copy-start.4 = (bf16[64,3072]{1,0:T(8,128)(2,1)S(1)}, bf16[64,3072]{1,0:T(8,128)(2,1)}, u32[]{:S(2)}) copy-start(bf16[64,3072]{1,0:T(8,128)(2,1)} %embed_ref.3) | copy-start | bytes 1179652
  9.5 1.4 copy-start.21
  17.6 1.0 copy-start.7
  18.5 0.8 copy-start.16
  46.4 0.7 copy-start.8
  47.1 0.6 copy-start.17
  49.2 1.0 copy-start.9
  50.2 0.9 copy-start.11
  51.1 0.8 copy-start.18
  53.3 39.2 %copy-start.22 = (s32[192]{0:T(256)S(1)}, s32[192]{0:T(256)}, u32[]{:S(2)}) copy-start(s32[192]{0:T(256)} %param.15) | copy-start | bytes 2308
  53.3 40.0 %copy-start.19 = (f32[128]{0:T(128)S(1)}, f32[128]{0:T(128)}, u32[]{:S(2)}) copy-start(f32[128]{0:T(128)} %param.20) | copy-start | bytes 1540
  53.3 40.0 %copy-start.20 = (f32[128]{0:T(128)S(1)}, f32[128]{0:T(128)}, u32[]{:S(2)}) copy-start(f32[128]{0:T(128)} %param.21) | copy-start | bytes 1540
  90.6 1.9 %copy-start.1 = (bf16[2,32,128,256]{3,2,1,0:T(8,128)(2,1)}, bf16[2,32,128,256]{3,2,1,0:T(8,128)(2,1)S(1)}, u32[]{:S(2)}) copy-start(bf16[2,32,128,256]{3,2,1,0:T(8,128)(2,1)S(1)} %shard_map.133.slots) | copy-start | bytes 12582916
  93.3 2.2 %copy-start.2 = (bf16[2,32,128,256]{3,2,1,0:T(8,128)(2,1)S(1)}, bf16[2,32,128,256]{3,2,1,0:T(8,128)(2,1)}, u32[]{:S(2)}) copy-start(bf16[2,32,128,256]{3,2,1,0:T(8,128)(2,1)} %copy-done.1) | copy-start | bytes 12582916
  95.5 1.0 copy-start.10
  96.4 0.9 copy-start.12
  117.0 14.8 %copy-start.13 = (bf16[192,64]{1,0:T(8,128)(2,1)}, bf16[192,64]{1,0:T(8,128)(2,1)S(1)}, u32[]{:S(2)}) copy-start(bf16[192,64]{1,0:T(8,128)(2,1)S(1)} %get-tuple-element.16.lat_ref) | copy-start | bytes 73732
  131.8 0.8 copy-start.5
  133.4 2.2 %copy-start.3 = (bf16[2,32,128,256]{3,2,1,0:T(8,128)(2,1)S(1)}, bf16[2,32,128,256]{3,2,1,0:T(8,128)(2,1)}, u32[]{:S(2)}) copy-start(bf16[2,32,128,256]{3,2,1,0:T(8,128)(2,1)} %copy-done.1) | copy-start | bytes 12582916
  135.6 1.0 copy-start.6
  136.6 0.8 copy-start.14
  137.4 1.5 %copy-start.15 = (bf16[192,64]{1,0:T(8,128)(2,1)S(1)}, bf16[192,64]{1,0:T(8,128)(2,1)}, u32[]{:S(2)}) copy-start(bf16[192,64]{1,0:T(8,128)(2,1)} %copy-done.13) | copy-start | bytes 73732

commit v2 on v0

v2 whole, which is shorter than its diff:
```python
import jax
import jax.numpy as jnp
from jax import lax
from jax.experimental import pallas as pl
from jax.experimental.pallas import tpu as pltpu
from jax.sharding import PartitionSpec as P

MESH = pl.DeviceIdType.MESH
HD = 128
HEADS = 3
LAT = 64
ROWS = 192
LANES = 256
WID = HEADS * HD
DIM = 3072
FEAT = 80
CHUNK = 768
CHUNKS = 16
STEP = 8
MCOLS = 48
QUARTER = 768
PARTS = 4
DEPTH = DIM // PARTS
F32 = jnp.float32
BF16 = jnp.bfloat16
NT = (((1,), (1,)), ((), ()))
NN = (((1,), (0,)), ((), ()))
TN = (((0,), (0,)), ((), ()))
EPS = 1e-6
LOG2E = 1.4426950408889634
VMEM_LIMIT = 58 * 1024 * 1024


def dot(a, b, dims):
    return lax.dot_general(a, b, dims, preferred_element_type=F32)


def split(value):
    high = value.astype(BF16).astype(F32)
    return high, value - high


def kernel(
    pixels, w_encode, w_latent, source, w_embed, mod_shift, mod_scale, gate, q_gain, k_gain, w_qkv, w_out,
    lat_out, block_out,
    pix_v, enc_v, wlat_v, src_v, emb_v, shift_v, scale_v, gate_v, qg_v, kg_v, wqkv_v, wout_v,
    wide, wp, lat_in, core_in, half, x_in, y_in, weights,
    slots, m_in, m_slots, latq, square, queries, keys, vals, s_even, s_odd, running, top, accum,
    first, second, assembled,
    load, send, recv,
):
    s = lax.axis_index("sec")
    t = lax.axis_index("tp")
    z = s // 32
    x = (s // 8) % 4
    y = (s // 2) % 4
    c = s % 2
    u = x + c * (y - x)
    v = y + c * (x - y)
    b = z * 4 + y
    at = (v * 4 + u) * 2 + z
    sibling = {"sec": s + 1 - 2 * c}
    tp_peers = [{"tp": (t + k) % 4} for k in range(1, 4)]
    x_at = [(x + k) % 4 for k in range(1, 4)]
    x_peers = [{"sec": s + (xx - x) * 8} for xx in x_at]
    b_at = [(b + k) % 8 for k in range(1, 8)]
    b_peers = [{"sec": (bb // 4) * 32 + x * 8 + (bb % 4) * 2 + c} for bb in b_at]
    z_peer = {"sec": s + (1 - 2 * z) * 32}
    u_peers = [{"sec": s + ((u + k) % 4 - u) * (8 - 6 * c)} for k in range(1, 4)]
    v_peers = [{"sec": s + ((v + k) % 4 - v) * (2 + 6 * c)} for k in range(1, 4)]
    m_to = {"tp": s // 16, "sec": ((s % 16) * 4 + t + 1) % 64}
    back = (s + 63) % 64
    m_from = {"tp": back % 4, "sec": t * 16 + back // 4}

    sent = []
    used = [0]

    def push(src, dst, device):
        i = used[0]
        used[0] += 1
        copy = pltpu.make_async_remote_copy(
            src_ref=src, dst_ref=dst, send_sem=send.at[i], recv_sem=recv.at[i], device_id=device, device_id_type=MESH
        )
        copy.start()
        sent.append(copy)
        return copy

    loads = [0]

    def fetch(src, dst):
        copy = pltpu.make_async_copy(src, dst, load.at[loads[0]])
        loads[0] += 1
        copy.start()
        return copy

    early = [fetch(w_embed, emb_v), fetch(w_qkv, wqkv_v), fetch(mod_scale, scale_v), fetch(mod_shift, shift_v)]
    parts = []
    for k in range(PARTS):
        depth = pl.ds(k * DEPTH, DEPTH)
        parts.append((fetch(pixels.at[:, depth], pix_v.at[k]), fetch(w_encode.at[depth], enc_v.at[k])))
    wlat_load = fetch(w_latent, wlat_v)
    late = [
        fetch(source, src_v), fetch(gate, gate_v), fetch(q_gain, qg_v), fetch(k_gain, kg_v), fetch(w_out, wout_v)
    ]

    barrier = pltpu.get_barrier_semaphore()
    greet = tp_peers + [sibling] + x_peers + b_peers + [m_from]
    for device in greet:
        pl.semaphore_signal(barrier, inc=1, device_id=device, device_id_type=MESH)

    for copy in early:
        copy.wait()
    block = (3 * s) // 8 - s // 62
    base = pl.ds(pl.multiple_of(block * HD, HD), LANES)
    mean = jnp.mean(emb_v[...].astype(F32), axis=1, keepdims=True)
    wide[0:LAT, :] = (emb_v[:, base].astype(F32) - mean) * scale_v[:, base]
    wide[LAT:HD, :] = jnp.where(
        lax.broadcasted_iota(jnp.int32, (LAT, LANES), 0) == 0, jnp.broadcast_to(shift_v[:, base], (LAT, LANES)), 0.0
    )
    offset = s * MCOLS - block * HD
    turned = pltpu.roll(wide[...], (LANES - offset) % LANES, 1)[:, 0:HD].T
    high, low = split(turned[0:MCOLS, :])
    high, low = high.astype(BF16), low.astype(BF16)
    for i in range(3):
        wp[i * WID : (i + 1) * WID, :] = (dot(wqkv_v[i], high, TN) + dot(wqkv_v[i], low, TN)).astype(BF16)

    pl.semaphore_wait(barrier, len(greet))
    mine = pl.ds(pl.multiple_of(c * 576, 576), 576)
    other = pl.ds(pl.multiple_of((1 - c) * 576, 576), 576)
    w_core = push(wp.at[other], core_in, sibling)

    total = jnp.zeros((ROWS, 512), F32)
    for k in range(PARTS):
        parts[k][0].wait()
        parts[k][1].wait()
        total += dot(pix_v[k], enc_v[k], NN)
    hidden = jax.nn.silu(total).astype(BF16)
    wlat_load.wait()
    wide[...] = jnp.zeros_like(wide)
    wide[0:LAT, 0:ROWS] = dot(wlat_v[...], hidden, NT)
    lat_in[t] = pltpu.roll(wide[0:LAT, :], LAT * c, 1).astype(BF16)
    lat_tp = [push(lat_in.at[t], lat_in.at[t], device) for device in tp_peers]

    w_core.wait_recv()
    half[...] = (wp[mine, :].astype(F32) + core_in[...].astype(F32)).astype(BF16)
    w_x = []
    for k in range(3):
        w_x.append(push(half.at[pl.ds(pl.multiple_of(x_at[k] * 144, 144), 144)], x_in.at[x], x_peers[k]))
    x_in[x] = half[pl.ds(pl.multiple_of(x * 144, 144), 144), :]

    for copy in lat_tp:
        copy.wait_recv()
    summed = lat_in[0].astype(F32)
    for k in range(1, 4):
        summed += lat_in[k].astype(F32)
    lat = summed.astype(BF16)
    embedded = dot(emb_v[...], lat, TN)
    center = embedded - jnp.mean(embedded, axis=0, keepdims=True)
    rstd = lax.rsqrt(jnp.mean(center * center, axis=0, keepdims=True) + EPS)
    rstd = jnp.broadcast_to(rstd, (LAT, LANES))
    row = lax.broadcasted_iota(jnp.int32, (LAT, LANES), 0)
    lane = lax.broadcasted_iota(jnp.int32, (LAT, LANES), 1)
    high, low = split(rstd)
    piece = lat.astype(F32)
    spare = (lane >= ROWS * (1 - c)) & (lane < ROWS * (1 - c) + LAT)
    for k in range(3):
        turn = (ROWS * (1 - c) - LAT * c - LAT * k + 2 * LANES) % LANES
        piece = jnp.where(spare & (row == k), pltpu.roll(high, turn, 1), piece)
        piece = jnp.where(spare & (row == k + 3), pltpu.roll(low, turn, 1), piece)
    slots[c, at] = piece.astype(BF16)
    lat_z = push(slots.at[c, at], slots.at[c, at], z_peer)

    for copy in w_x:
        copy.wait_recv()
    added = x_in[0].astype(F32)
    for k in range(1, 4):
        added += x_in[k].astype(F32)
    y_in[b] = added.astype(BF16)
    w_b = [push(y_in.at[b], y_in.at[b], device) for device in b_peers]

    lat_z.wait_recv()
    pair = pl.ds((v * 4 + u) * 2, 2)
    lat_u = [push(slots.at[c, pair], slots.at[c, pair], device) for device in u_peers]

    for copy in w_b:
        copy.wait_recv()
    added = y_in[0].astype(F32)
    for k in range(1, 8):
        added += y_in[k].astype(F32)
    place = pl.ds(pl.multiple_of(c * 576 + x * 144, 144), 144)
    weights[place, :] = added.astype(BF16)
    w_g = [push(weights.at[place], weights.at[place], device) for device in x_peers]

    for copy in lat_u:
        copy.wait_recv()
    group = pl.ds(v * 8, 8)
    lat_v = [push(slots.at[c, group], slots.at[c, group], device) for device in v_peers]
    lat_c = [push(slots.at[c, group], slots.at[c, group], sibling)]

    for copy in w_g:
        copy.wait_recv()
    w_last = push(weights.at[mine], weights.at[mine], sibling)
    for copy in late:
        copy.wait()
    square[...] = jnp.zeros_like(square)
    square[:, 0:ROWS] = jnp.broadcast_to(src_v[...].astype(F32), (HD, ROWS))
    origin = square[...].T[0:ROWS, 0:1].astype(jnp.int32)
    latq[...] = jnp.zeros_like(latq)
    w_last.wait_recv()

    wide_m = lax.broadcasted_iota(jnp.int32, (MCOLS, HD), 1)
    terms = [
        dot(wout_v[:, h * HD : (h + 1) * HD], weights[2 * WID + h * HD : 2 * WID + (h + 1) * HD, :], NN)
        for h in range(HEADS)
    ]
    m_in[0, :, 0:HD] = jnp.where(wide_m < LAT, terms[0], pltpu.roll(terms[1], LAT, 1)).astype(BF16)
    m_in[0, :, HD:LANES] = jnp.where(wide_m < LAT, terms[2], terms[0] + terms[1] + terms[2]).astype(BF16)
    m_move = push(m_in.at[0], m_in.at[1], m_to)

    lane_t = lax.broadcasted_iota(jnp.int32, (1, HD), 1)
    lane_c = lax.broadcasted_iota(jnp.int32, (1, CHUNK), 1)
    tail_row = lax.broadcasted_iota(jnp.int32, (16, CHUNK), 0)

    def prepare(k, g0, g1):
        def one(i, carry):
            lats, scales = [], []
            for zz in range(2):
                left = slots[0, g0 * 8 + 2 * i + zz]
                right = slots[1, g1 * 8 + 2 * i + zz]
                middle = jnp.where(lane_t < LAT, left[:, HD:].astype(F32), right[:, :HD].astype(F32))
                lats += [left[:, :HD].astype(F32), middle, right[:, HD:].astype(F32)]
                sl = left[0:16, HD:].astype(F32)
                sr = right[0:16, :HD].astype(F32)
                sl = sl[0:3] + sl[3:6]
                sr = sr[0:3] + sr[3:6]
                tl = pltpu.roll(sl, LAT, 1)
                tr = pltpu.roll(sr, LAT, 1)
                scales += [
                    jnp.where(lane_t < LAT, tl[0:1], sl[1:2]),
                    jnp.where(lane_t < LAT, tl[2:3], tr[0:1]),
                    jnp.where(lane_t < LAT, sr[1:2], tr[2:3]),
                ]
            lat_c32 = jnp.concatenate(lats, axis=1)
            scale_row = jnp.concatenate(scales, axis=1)
            lat_cb = lat_c32.astype(BF16)
            upper = lane_c // 384
            inner = lane_c - upper * 384
            base0 = i * 8 * ROWS + g0 * 2 * ROWS
            base1 = g1 * 8 * ROWS + i * 2 * ROWS + ROWS
            token = inner + upper * (32 * ROWS) + jnp.where(inner < ROWS, base0, base1 - ROWS)
            hit = jnp.where(origin == token, 1.0, 0.0).astype(BF16)
            latq[0:ROWS, 0:LAT] += dot(hit, lat_cb, NT)
            n = 4 * k + i
            scaled = lat_c32 * scale_row
            vals[n, 0:LAT, :] = scaled.astype(BF16)
            vals[n, LAT:FEAT, :] = jnp.where(tail_row == 0, 1.0, 0.0).astype(BF16)
            for h in range(HEADS):
                wk = weights[WID + h * HD : WID + (h + 1) * HD, :]
                raw = dot(wk[:, 0:LAT], lat_cb, NN) * scale_row + wk[:, LAT : LAT + 1].astype(F32)
                inv = lax.rsqrt(jnp.mean(raw * raw, axis=0, keepdims=True) + EPS)
                ih, il = split(inv)
                tail = jnp.where((tail_row == 0) | (tail_row == 2), ih, 0.0)
                tail = jnp.where(tail_row == 1, il, tail)
                keys[h, n, 0:LAT, :] = (scaled * inv).astype(BF16)
                keys[h, n, LAT:FEAT, :] = tail.astype(BF16)
            return carry

        lax.fori_loop(0, 4, one, 0)

    for k in range(4):
        if k:
            lat_v[k - 1].wait_recv()
            came = pl.ds(((v + 4 - k) % 4) * 8, 8)
            lat_c.append(push(slots.at[c, came], slots.at[c, came], sibling))
        lat_c[k].wait_recv()
        prepare(k, (y + 4 - k) % 4, (x + 4 - k) % 4)
        if k == 1:
            m_move.wait_recv()
            m_slots[c, at] = m_in[1]
            m_z = push(m_slots.at[c, at], m_slots.at[c, at], z_peer)
    m_z.wait_recv()
    m_u = [push(m_slots.at[c, pair], m_slots.at[c, pair], device) for device in u_peers]

    rows = latq[0:ROWS, :].astype(BF16)
    lat_out[...] = latq[...].T[0:LAT, 0:ROWS].astype(BF16)
    embedded = dot(rows[:, 0:LAT], emb_v[...], NN)
    center = embedded - jnp.mean(embedded, axis=1, keepdims=True)
    rstd = lax.rsqrt(jnp.mean(center * center, axis=1, keepdims=True) + EPS)
    unit = jnp.where(lax.broadcasted_iota(jnp.int32, (16, HD), 1) == LAT, 1.0, 0.0).astype(BF16)
    lane_q = lax.broadcasted_iota(jnp.int32, (ROWS, HD), 1)
    for h in range(HEADS):
        wq = weights[h * HD : (h + 1) * HD, :]
        wk = weights[WID + h * HD : WID + (h + 1) * HD, :]
        raw = rstd * dot(rows, wq, NT) + dot(unit, wq, NT)[0:1, :]
        q = raw * lax.rsqrt(jnp.mean(raw * raw, axis=1, keepdims=True) + EPS) * qg_v[...]
        high, low = split(q * kg_v[...] * (LOG2E / HD**0.5))
        folded = dot(high.astype(BF16), wk, NN) + dot(low.astype(BF16), wk, NN)
        bias_high, bias_low = split(folded[:, LAT : LAT + 1])
        value = jnp.where(lane_q < LAT, folded, 0.0)
        value = jnp.where((lane_q == LAT) | (lane_q == LAT + 1), bias_high, value)
        value = jnp.where(lane_q == LAT + 2, bias_low, value)
        queries[h] = value.astype(BF16)

    scores = [s_even, s_odd]
    running[...] = jnp.full_like(running, -jnp.inf)
    accum[...] = jnp.zeros_like(accum)

    def score(i, h):
        most = running[h]
        for j in range(STEP):
            n = i * STEP + j
            part = dot(queries[h][:, 0:FEAT], keys[h, n], NN)
            scores[h % 2][n] = part
            for k in range(CHUNK // HD):
                most = jnp.maximum(most, part[:, k * HD : (k + 1) * HD])
        running[h] = most

    def weigh(i, h):
        most = top[h]
        added = accum[h, :, 0:FEAT]
        for j in range(STEP):
            n = i * STEP + j
            w = jnp.concatenate(
                [jnp.exp2(scores[h % 2][n, :, k * HD : (k + 1) * HD] - most).astype(BF16) for k in range(CHUNK // HD)],
                axis=1,
            )
            added += dot(w, vals[n], NT)
        accum[h, :, 0:FEAT] = added

    def start(i, carry):
        score(i, 0)
        return carry

    lax.fori_loop(0, CHUNKS // STEP, start, 0)
    for copy in m_u:
        copy.wait_recv()
    m_v = [push(m_slots.at[c, group], m_slots.at[c, group], device) for device in v_peers]
    m_c = [push(m_slots.at[c, group], m_slots.at[c, group], sibling)]
    mixed = []
    for h in range(HEADS):
        top[h] = jnp.broadcast_to(jnp.max(running[h], axis=1, keepdims=True), (ROWS, HD))

        def both(i, carry):
            weigh(i, h)
            if h + 1 < HEADS:
                score(i, h + 1)
            return carry

        lax.fori_loop(0, CHUNKS // STEP, both, 0)
        mixed.append(accum[h] / accum[h, :, LAT : LAT + 1])
        if h == 1:
            first[t] = jnp.where(lane_q < LAT, mixed[0], pltpu.roll(mixed[1], LAT, 1)).astype(BF16)
            o_first = [push(first.at[t], first.at[t], device) for device in tp_peers]
            for k in range(1, 4):
                m_v[k - 1].wait_recv()
                came = pl.ds(((v + 4 - k) % 4) * 8, 8)
                m_c.append(push(m_slots.at[c, came], m_slots.at[c, came], sibling))
    lower = pltpu.roll(mixed[2][ROWS // 2 :, :], LAT, 1)
    second[t] = jnp.where(lane_q[0 : ROWS // 2] < LAT, mixed[2][0 : ROWS // 2, :], lower).astype(BF16)
    o_second = [push(second.at[t], second.at[t], device) for device in tp_peers]

    for copy in m_c:
        copy.wait_recv()
    for slot in range(64):
        cc, rest = slot // 32, slot % 32
        vv, uu, zz = rest // 8, (rest // 2) % 4, rest % 2
        xx, yy = (uu, vv) if cc == 0 else (vv, uu)
        origin_at = (zz * 32 + xx * 8 + yy * 2 + cc + 63) % 64
        assembled[origin_at % 4, pl.ds((origin_at // 4) * MCOLS, MCOLS), :] = m_slots[cc, rest]
    quarter = pl.ds(pl.multiple_of(t * QUARTER, QUARTER), QUARTER)
    embedded = dot(rows[:, 0:LAT], emb_v[:, quarter], NN)
    for copy in o_first:
        copy.wait_recv()
    total = dot(first[0], assembled[0, :, 0:HD], NT)
    for k in range(1, 4):
        total += dot(first[k], assembled[k, :, 0:HD], NT)
    for copy in o_second:
        copy.wait_recv()
    one = jnp.where(lane_q == LAT, 1.0, 0.0)
    for k in range(4):
        packed = second[k].astype(F32)
        whole = jnp.concatenate([packed, pltpu.roll(packed, LAT, 1)], axis=0)
        whole = jnp.where(lane_q < LAT, whole, one).astype(BF16)
        total += dot(whole, assembled[k, :, HD:LANES], NT)
    block_out[...] = (embedded + gate_v[:, quarter] * total).astype(BF16)
    for copy in sent:
        copy.wait_send()


COPIES = 47
LOADS = 18


def per_device(
    pixels, w_encode, w_latent, source_row, w_embed, mod_shift, mod_scale, gate, q_gain, k_gain, w_qkv, w_out
):
    operands = (
        pixels, w_encode, w_latent.T, source_row.reshape(1, ROWS), w_embed, mod_shift.reshape(1, DIM),
        mod_scale.reshape(1, DIM), gate.reshape(1, DIM), q_gain.reshape(1, HD), k_gain.reshape(1, HD), w_qkv, w_out.T,
    )
    vmem = pltpu.VMEM
    scratch = [
        vmem((PARTS, ROWS, DEPTH), BF16),
        vmem((PARTS, DEPTH, 512), BF16),
        vmem((LAT, 512), BF16),
        vmem((1, ROWS), jnp.int32),
        vmem((LAT, DIM), BF16),
        vmem((1, DIM), F32),
        vmem((1, DIM), F32),
        vmem((1, DIM), F32),
        vmem((1, HD), F32),
        vmem((1, HD), F32),
        vmem((3, MCOLS, WID), BF16),
        vmem((MCOLS, WID), BF16),
        vmem((HD, LANES), F32),
        vmem((3 * WID, HD), BF16),
        vmem((4, LAT, LANES), BF16),
        vmem((576, HD), BF16),
        vmem((576, HD), BF16),
        vmem((4, 144, HD), BF16),
        vmem((8, 144, HD), BF16),
        vmem((3 * WID, HD), BF16),
        vmem((2, 32, LAT, LANES), BF16),
        vmem((2, MCOLS, LANES), BF16),
        vmem((2, 32, MCOLS, LANES), BF16),
        vmem((LANES, HD), F32),
        vmem((HD, LANES), F32),
        vmem((HEADS, ROWS, HD), BF16),
        vmem((HEADS, CHUNKS, FEAT, CHUNK), BF16),
        vmem((CHUNKS, FEAT, CHUNK), BF16),
        vmem((CHUNKS, ROWS, CHUNK), F32),
        vmem((CHUNKS, ROWS, CHUNK), F32),
        vmem((HEADS, ROWS, HD), F32),
        vmem((HEADS, ROWS, HD), F32),
        vmem((HEADS, ROWS, HD), F32),
        vmem((4, ROWS, HD), BF16),
        vmem((4, ROWS // 2, HD), BF16),
        vmem((4, QUARTER, LANES), BF16),
        pltpu.SemaphoreType.DMA((LOADS,)),
        pltpu.SemaphoreType.DMA((COPIES,)),
        pltpu.SemaphoreType.DMA((COPIES,)),
    ]
    lat, out = pl.pallas_call(
        kernel,
        out_shape=(jax.ShapeDtypeStruct((LAT, ROWS), BF16), jax.ShapeDtypeStruct((ROWS, QUARTER), BF16)),
        in_specs=[pl.BlockSpec(memory_space=pl.ANY)] * len(operands),
        out_specs=(pl.BlockSpec(memory_space=pltpu.VMEM), pl.BlockSpec(memory_space=pltpu.VMEM)),
        scratch_shapes=scratch,
        compiler_params=pltpu.CompilerParams(collective_id=0, has_side_effects=True, vmem_limit_bytes=VMEM_LIMIT),
    )(*operands)
    return lat.T, out


def solution(mesh):
    placed = (
        P("sec", None), P(None, "tp"), P("tp", None), P("sec"), P(), P(), P(), P(), P(), P(),
        P(None, "sec", "tp"), P("tp", "sec"),
    )
    return jax.shard_map(
        per_device, mesh=mesh, in_specs=placed, out_specs=(P("sec", None), P("sec", "tp")), check_vma=False
    )
```

time: 672 us -> 69.2 us (0.10)
  waiting for transfers between devices: 467 us -> 0 us
  local copies, waits for them, and re-layouts: 84.1 us -> 3.07 us
  matrix products: 69.3 us -> 0 us
  Pallas kernels: 0 us -> 65.2 us
  blocking collectives: 20.1 us -> 0 us
  other arithmetic: 14.7 us -> 0 us
  between operations: 14.3 us -> 0.64 us
    all_gather x5 -> x0, waiting for transfers between devices: 433 us -> none  [the longest x1 116 us: per_device(): lax.all_gather(valrow, 'sec', axis=0, tiled=True)]
    dot_general x20 -> x0, matrix products: 69.3 us -> none  [the longest x8 30.4 us: attend_block(): jnp.einsum('thd,nhd->htn', query, keys_in, preferred_element_type=jnp.flo...]
    dynamic_slice x25 -> x0, local copies, waits for them, and re-layouts: 65.5 us -> none  [the longest x24 64.7 us: per_device(): carry, unused = lax.scan(attend_block, carry, (keys_all, vals_all))]
    pallas_call x0 -> x1, Pallas kernels: none -> 65.2 us  [per_device(): pl.pallas_call(kernel, out_shape=(jax.ShapeDtypeStruct((LAT, ROWS), BF16)...]
    reduce_scatter x1 -> x0, waiting for transfers between devices: 33.1 us -> none  [per_device(): lax.psum_scatter(terms.astype(jnp.bfloat16), 'tp', scatter_dimension=1, t...]
    psum x1 -> x0, blocking collectives: 20.1 us -> none  [per_device(): encoded = lax.psum(partial_lat.astype(jnp.bfloat16), 'tp')]
    reduce_sum x11 -> x0, other arithmetic: 7.65 us -> none  [the longest x8 5.08 us: attend_block(): totals = totals * shrink + jnp.sum(expos, axis=2)]
  transfers between devices with their start and end apart: 6 -> 0, of which waited for: 5 -> 0; matrix products, arithmetic and copies ran while one was open for 21% -> 0% of each run, Pallas kernels for 0% -> 0%
where the time goes in v2:
time: 69.2 us; the launch traced here: 68.9 us
  Pallas kernels  65.2 us (94%)
  local copies, waits for them, and re-layouts  3.07 us (4%)
    pallas_call x1, Pallas kernels, per_device(): pl.pallas_call(kernel, out_shape=(jax.ShapeDtypeStruct((LAT, ROWS), BF16)...  65.2 us
    unnamed x2, local copies, waits for them, and re-layouts  3.07 us

profile of v2, /device:TPU:1, one launch (start us, length us, event | category | flops | bytes accessed | tf_op | source)
XLA Modules:
  0.0 68.9 jit_solution(3861385314337327139)
XLA Ops:
  0.6 65.2 %shard_map.131 = (bf16[64,192]{1,0:T(8,128)(2,1)}, bf16[192,768]{1,0:T(8,128)(2,1)}) custom-call(bf16[192,3072]{1,0:T(8,128)(2,1)} %pixels.1, bf16[3072,512]{1,0:T(8,128)(2,1)} %w_encode.1, bf16[64,512]{1,0:T(8,128)(2,1)} %bitcast.9, s32[1,192]{1,0:T(1,128)} %bitcast.15, bf16[64,3072]{1,0:T(8,128)(2,1)} %w_embed.1, f32[1,3072]{1,0:T(1,128)} %bitcast.12, ...), custom_call_target="tpu_custom_call" | custom-call | tf_op jit(solution)/shard_map/pallas_call | solution.py:443
  65.8 1.4 %copy.16 = bf16[192,64]{0,1:T(8,128)(2,1)} copy(bf16[192,64]{0,1:T(8,128)(2,1)} %bitcast.11) | data formatting | bytes 49152
  67.2 1.7 %copy.17 = bf16[192,768]{1,0:T(8,128)(2,1)} copy(bf16[192,768]{1,0:T(8,128)(2,1)} %get-tuple-element.9) | data formatting | bytes 589824

commit v3 on v2

--- a/solution.py
+++ b/solution.py
@@ -16,7 +16,6 @@
 FEAT = 80
 CHUNK = 768
 CHUNKS = 16
-STEP = 8
 MCOLS = 48
 QUARTER = 768
 PARTS = 4
@@ -44,7 +43,7 @@
     pixels, w_encode, w_latent, source, w_embed, mod_shift, mod_scale, gate, q_gain, k_gain, w_qkv, w_out,
     lat_out, block_out,
     pix_v, enc_v, wlat_v, src_v, emb_v, shift_v, scale_v, gate_v, qg_v, kg_v, wqkv_v, wout_v,
-    wide, wp, lat_in, core_in, half, x_in, y_in, weights,
+    wide, centred, centred_t, wp, lat_in, core_in, half, x_in, y_in, weights,
     slots, m_in, m_slots, latq, square, queries, keys, vals, s_even, s_odd, running, top, accum,
     first, second, assembled,
     load, send, recv,
@@ -115,7 +114,7 @@
     mean = jnp.mean(emb_v[...].astype(F32), axis=1, keepdims=True)
     wide[0:LAT, :] = (emb_v[:, base].astype(F32) - mean) * scale_v[:, base]
     wide[LAT:HD, :] = jnp.where(
-        lax.broadcasted_iota(jnp.int32, (LAT, LANES), 0) == 0, jnp.broadcast_to(shift_v[:, base], (LAT, LANES)), 0.0
+        lax.broadcasted_iota(jnp.int32, (LAT, LANES), 0) < 2, jnp.broadcast_to(shift_v[:, base], (LAT, LANES)), 0.0
     )
     offset = s * MCOLS - block * HD
     turned = pltpu.roll(wide[...], (LANES - offset) % LANES, 1)[:, 0:HD].T
@@ -123,11 +122,6 @@
     high, low = high.astype(BF16), low.astype(BF16)
     for i in range(3):
         wp[i * WID : (i + 1) * WID, :] = (dot(wqkv_v[i], high, TN) + dot(wqkv_v[i], low, TN)).astype(BF16)
-
-    pl.semaphore_wait(barrier, len(greet))
-    mine = pl.ds(pl.multiple_of(c * 576, 576), 576)
-    other = pl.ds(pl.multiple_of((1 - c) * 576, 576), 576)
-    w_core = push(wp.at[other], core_in, sibling)
 
     total = jnp.zeros((ROWS, 512), F32)
     for k in range(PARTS):
@@ -139,7 +133,17 @@
     wide[...] = jnp.zeros_like(wide)
     wide[0:LAT, 0:ROWS] = dot(wlat_v[...], hidden, NT)
     lat_in[t] = pltpu.roll(wide[0:LAT, :], LAT * c, 1).astype(BF16)
+
+    pl.semaphore_wait(barrier, len(greet))
+    mine = pl.ds(pl.multiple_of(c * 576, 576), 576)
+    other = pl.ds(pl.multiple_of((1 - c) * 576, 576), 576)
+    w_core = push(wp.at[other], core_in, sibling)
     lat_tp = [push(lat_in.at[t], lat_in.at[t], device) for device in tp_peers]
+
+    high, low = split(emb_v[...].astype(F32) - mean)
+    both_terms = jnp.concatenate([high, low], axis=0)
+    centred[...] = both_terms.astype(BF16)
+    centred_t[...] = both_terms.T.astype(BF16)
 
     w_core.wait_recv()
     half[...] = (wp[mine, :].astype(F32) + core_in[...].astype(F32)).astype(BF16)
@@ -148,15 +152,25 @@
         w_x.append(push(half.at[pl.ds(pl.multiple_of(x_at[k] * 144, 144), 144)], x_in.at[x], x_peers[k]))
     x_in[x] = half[pl.ds(pl.multiple_of(x * 144, 144), 144), :]
 
+    for copy in late:
+        copy.wait()
+    square[...] = jnp.zeros_like(square)
+    square[:, 0:ROWS] = jnp.broadcast_to(src_v[...].astype(F32), (HD, ROWS))
+    origin = square[...].T[0:ROWS, 0:1].astype(jnp.int32)
+    latq[...] = jnp.zeros_like(latq)
+
     for copy in lat_tp:
         copy.wait_recv()
     summed = lat_in[0].astype(F32)
     for k in range(1, 4):
         summed += lat_in[k].astype(F32)
     lat = summed.astype(BF16)
-    embedded = dot(emb_v[...], lat, TN)
-    center = embedded - jnp.mean(embedded, axis=0, keepdims=True)
-    rstd = lax.rsqrt(jnp.mean(center * center, axis=0, keepdims=True) + EPS)
+    twice = jnp.concatenate([lat, lat], axis=0)
+    squares = jnp.zeros((1, LANES), F32)
+    for k in range(PARTS):
+        center = dot(centred_t[k * DEPTH : (k + 1) * DEPTH, :], twice, NN)
+        squares += jnp.sum(center * center, axis=0, keepdims=True)
+    rstd = lax.rsqrt(squares * (1.0 / DIM) + EPS)
     rstd = jnp.broadcast_to(rstd, (LAT, LANES))
     row = lax.broadcasted_iota(jnp.int32, (LAT, LANES), 0)
     lane = lax.broadcasted_iota(jnp.int32, (LAT, LANES), 1)
@@ -194,18 +208,24 @@
     for copy in lat_u:
         copy.wait_recv()
     group = pl.ds(v * 8, 8)
-    lat_v = [push(slots.at[c, group], slots.at[c, group], device) for device in v_peers]
-    lat_c = [push(slots.at[c, group], slots.at[c, group], sibling)]
+    right, left = v_peers[0], v_peers[2]
+
+    def halves(which):
+        return [pl.ds(which * 8, 4), pl.ds(which * 8 + 4, 4)]
+
+    def forward(place, device):
+        return push(slots.at[c, place], slots.at[c, place], device)
+
+    own_a, own_b = halves(v)
+    right_a = forward(own_a, right)
+    left_b = forward(own_b, left)
+    right_b = forward(own_b, right)
+    left_a = forward(own_a, left)
+    lat_c = [forward(group, sibling)]
 
     for copy in w_g:
         copy.wait_recv()
     w_last = push(weights.at[mine], weights.at[mine], sibling)
-    for copy in late:
-        copy.wait()
-    square[...] = jnp.zeros_like(square)
-    square[:, 0:ROWS] = jnp.broadcast_to(src_v[...].astype(F32), (HD, ROWS))
-    origin = square[...].T[0:ROWS, 0:1].astype(jnp.int32)
-    latq[...] = jnp.zeros_like(latq)
     w_last.wait_recv()
 
     wide_m = lax.broadcasted_iota(jnp.int32, (MCOLS, HD), 1)
@@ -222,15 +242,16 @@
     tail_row = lax.broadcasted_iota(jnp.int32, (16, CHUNK), 0)
 
     def prepare(k, g0, g1):
-        def one(i, carry):
+        for i in range(4):
+            n = 4 * k + i
             lats, scales = [], []
             for zz in range(2):
-                left = slots[0, g0 * 8 + 2 * i + zz]
-                right = slots[1, g1 * 8 + 2 * i + zz]
-                middle = jnp.where(lane_t < LAT, left[:, HD:].astype(F32), right[:, :HD].astype(F32))
-                lats += [left[:, :HD].astype(F32), middle, right[:, HD:].astype(F32)]
-                sl = left[0:16, HD:].astype(F32)
-                sr = right[0:16, :HD].astype(F32)
+                near = slots[0, g0 * 8 + 2 * i + zz]
+                far = slots[1, g1 * 8 + 2 * i + zz]
+                middle = jnp.where(lane_t < LAT, near[:, HD:].astype(F32), far[:, :HD].astype(F32))
+                lats += [near[:, :HD].astype(F32), middle, far[:, HD:].astype(F32)]
+                sl = near[0:16, HD:].astype(F32)
+                sr = far[0:16, :HD].astype(F32)
                 sl = sl[0:3] + sl[3:6]
                 sr = sr[0:3] + sr[3:6]
                 tl = pltpu.roll(sl, LAT, 1)
@@ -250,30 +271,40 @@
             token = inner + upper * (32 * ROWS) + jnp.where(inner < ROWS, base0, base1 - ROWS)
             hit = jnp.where(origin == token, 1.0, 0.0).astype(BF16)
             latq[0:ROWS, 0:LAT] += dot(hit, lat_cb, NT)
-            n = 4 * k + i
             scaled = lat_c32 * scale_row
             vals[n, 0:LAT, :] = scaled.astype(BF16)
             vals[n, LAT:FEAT, :] = jnp.where(tail_row == 0, 1.0, 0.0).astype(BF16)
+            high, low = split(1.0 / scale_row)
+            spread = jnp.where(tail_row == 0, high, 0.0)
+            spread = jnp.where(tail_row == 1, low, spread)
+            lat_x = jnp.concatenate([lat_cb, spread.astype(BF16)], axis=0)
             for h in range(HEADS):
-                wk = weights[WID + h * HD : WID + (h + 1) * HD, :]
-                raw = dot(wk[:, 0:LAT], lat_cb, NN) * scale_row + wk[:, LAT : LAT + 1].astype(F32)
-                inv = lax.rsqrt(jnp.mean(raw * raw, axis=0, keepdims=True) + EPS)
+                raw = dot(weights[WID + h * HD : WID + (h + 1) * HD, 0:FEAT], lat_x, NN)
+                power = jnp.mean(raw * raw, axis=0, keepdims=True)
+                inv = lax.rsqrt(power * (scale_row * scale_row) + EPS)
                 ih, il = split(inv)
                 tail = jnp.where((tail_row == 0) | (tail_row == 2), ih, 0.0)
                 tail = jnp.where(tail_row == 1, il, tail)
                 keys[h, n, 0:LAT, :] = (scaled * inv).astype(BF16)
                 keys[h, n, LAT:FEAT, :] = tail.astype(BF16)
-            return carry
-
-        lax.fori_loop(0, 4, one, 0)
-
-    for k in range(4):
+
+    for k, turn in enumerate((0, 1, 3, 2)):
+        came = (v + 4 - turn) % 4
+        if turn == 1:
+            right_a.wait_recv()
+            relay_a = forward(halves(came)[0], right)
+            left_b.wait_recv()
+            relay_b = forward(halves((v + 1) % 4)[1], left)
+            right_b.wait_recv()
+        elif turn == 3:
+            left_a.wait_recv()
+        elif turn == 2:
+            relay_a.wait_recv()
+            relay_b.wait_recv()
         if k:
-            lat_v[k - 1].wait_recv()
-            came = pl.ds(((v + 4 - k) % 4) * 8, 8)
-            lat_c.append(push(slots.at[c, came], slots.at[c, came], sibling))
+            lat_c.append(forward(pl.ds(came * 8, 8), sibling))
         lat_c[k].wait_recv()
-        prepare(k, (y + 4 - k) % 4, (x + 4 - k) % 4)
+        prepare(k, (y + 4 - turn) % 4, (x + 4 - turn) % 4)
         if k == 1:
             m_move.wait_recv()
             m_slots[c, at] = m_in[1]
@@ -283,9 +314,12 @@
 
     rows = latq[0:ROWS, :].astype(BF16)
     lat_out[...] = latq[...].T[0:LAT, 0:ROWS].astype(BF16)
-    embedded = dot(rows[:, 0:LAT], emb_v[...], NN)
-    center = embedded - jnp.mean(embedded, axis=1, keepdims=True)
-    rstd = lax.rsqrt(jnp.mean(center * center, axis=1, keepdims=True) + EPS)
+    twice = (latq[0:ROWS, :] + pltpu.roll(latq[0:ROWS, :], LAT, 1)).astype(BF16)
+    squares = jnp.zeros((ROWS, 1), F32)
+    for k in range(PARTS):
+        center = dot(twice, centred[:, k * DEPTH : (k + 1) * DEPTH], NN)
+        squares += jnp.sum(center * center, axis=1, keepdims=True)
+    rstd = lax.rsqrt(squares * (1.0 / DIM) + EPS)
     unit = jnp.where(lax.broadcasted_iota(jnp.int32, (16, HD), 1) == LAT, 1.0, 0.0).astype(BF16)
     lane_q = lax.broadcasted_iota(jnp.int32, (ROWS, HD), 1)
     for h in range(HEADS):
@@ -305,33 +339,24 @@
     running[...] = jnp.full_like(running, -jnp.inf)
     accum[...] = jnp.zeros_like(accum)
 
-    def score(i, h):
-        most = running[h]
-        for j in range(STEP):
-            n = i * STEP + j
-            part = dot(queries[h][:, 0:FEAT], keys[h, n], NN)
-            scores[h % 2][n] = part
-            for k in range(CHUNK // HD):
-                most = jnp.maximum(most, part[:, k * HD : (k + 1) * HD])
-        running[h] = most
-
-    def weigh(i, h):
-        most = top[h]
-        added = accum[h, :, 0:FEAT]
-        for j in range(STEP):
-            n = i * STEP + j
-            w = jnp.concatenate(
-                [jnp.exp2(scores[h % 2][n, :, k * HD : (k + 1) * HD] - most).astype(BF16) for k in range(CHUNK // HD)],
-                axis=1,
-            )
-            added += dot(w, vals[n], NT)
-        accum[h, :, 0:FEAT] = added
-
-    def start(i, carry):
-        score(i, 0)
-        return carry
-
-    lax.fori_loop(0, CHUNKS // STEP, start, 0)
+    def score(n, h, most):
+        part = dot(queries[h][:, 0:FEAT], keys[h, n], NN)
+        scores[h % 2][n] = part
+        for k in range(CHUNK // HD):
+            most = jnp.maximum(most, part[:, k * HD : (k + 1) * HD])
+        return most
+
+    def weigh(n, h, most):
+        w = jnp.concatenate(
+            [jnp.exp2(scores[h % 2][n, :, k * HD : (k + 1) * HD] - most).astype(BF16) for k in range(CHUNK // HD)],
+            axis=1,
+        )
+        return dot(w, vals[n], NT)
+
+    most = running[0]
+    for n in range(CHUNKS):
+        most = score(n, 0, most)
+    running[0] = most
     for copy in m_u:
         copy.wait_recv()
     m_v = [push(m_slots.at[c, group], m_slots.at[c, group], device) for device in v_peers]
@@ -340,13 +365,17 @@
     for h in range(HEADS):
         top[h] = jnp.broadcast_to(jnp.max(running[h], axis=1, keepdims=True), (ROWS, HD))
 
-        def both(i, carry):
-            weigh(i, h)
+        most = top[h]
+        added = accum[h, :, 0:FEAT]
+        if h + 1 < HEADS:
+            following = running[h + 1]
+        for n in range(CHUNKS):
             if h + 1 < HEADS:
-                score(i, h + 1)
-            return carry
-
-        lax.fori_loop(0, CHUNKS // STEP, both, 0)
+                following = score(n, h + 1, following)
+            added += weigh(n, h, most)
+        accum[h, :, 0:FEAT] = added
+        if h + 1 < HEADS:
+            running[h + 1] = following
         mixed.append(accum[h] / accum[h, :, LAT : LAT + 1])
         if h == 1:
             first[t] = jnp.where(lane_q < LAT, mixed[0], pltpu.roll(mixed[1], LAT, 1)).astype(BF16)
@@ -387,7 +416,18 @@
         copy.wait_send()
 
 
-COPIES = 47
+def leave(lat_ref, block_ref, lat_to, block_to, sem):
+    copies = [
+        pltpu.make_async_copy(lat_ref, lat_to, sem.at[0]),
+        pltpu.make_async_copy(block_ref, block_to, sem.at[1]),
+    ]
+    for copy in copies:
+        copy.start()
+    for copy in copies:
+        copy.wait()
+
+
+COPIES = 50
 LOADS = 18
 
 
@@ -413,6 +453,8 @@
         vmem((3, MCOLS, WID), BF16),
         vmem((MCOLS, WID), BF16),
         vmem((HD, LANES), F32),
+        vmem((HD, DIM), BF16),
+        vmem((DIM, HD), BF16),
         vmem((3 * WID, HD), BF16),
         vmem((4, LAT, LANES), BF16),
         vmem((576, HD), BF16),
@@ -448,6 +490,13 @@
         scratch_shapes=scratch,
         compiler_params=pltpu.CompilerParams(collective_id=0, has_side_effects=True, vmem_limit_bytes=VMEM_LIMIT),
     )(*operands)
+    lat, out = pl.pallas_call(
+        leave,
+        out_shape=(jax.ShapeDtypeStruct((LAT, ROWS), BF16), jax.ShapeDtypeStruct((ROWS, QUARTER), BF16)),
+        in_specs=[pl.BlockSpec(memory_space=pl.ANY)] * 2,
+        out_specs=(pl.BlockSpec(memory_space=pl.ANY), pl.BlockSpec(memory_space=pl.ANY)),
+        scratch_shapes=[pltpu.SemaphoreType.DMA((2,))],
+    )(lat, out)
     return lat.T, out
 
 

time: 69.2 us -> 73.1 us (1.056)
  Pallas kernels: 65.2 us -> 72.3 us
  local copies, waits for them, and re-layouts: 3.07 us -> 0 us
    pallas_call x0 -> x1, Pallas kernels: none -> 11 us  [per_device(): pl.pallas_call(leave, out_shape=(jax.ShapeDtypeStruct((LAT, ROWS), BF16),...]
    pallas_call x1, Pallas kernels: 65.2 us -> 61.2 us  [per_device(): pl.pallas_call(kernel, out_shape=(jax.ShapeDtypeStruct((LAT, ROWS), BF16)...]
    unnamed x2 -> x0, local copies, waits for them, and re-layouts: 3.07 us -> none
where the time goes in v3:
time: 73.1 us
  Pallas kernels  72.3 us (99%)
  between operations  0.8 us (1%)
    pallas_call x1, Pallas kernels, per_device(): pl.pallas_call(kernel, out_shape=(jax.ShapeDtypeStruct((LAT, ROWS), BF16)...  61.2 us
    pallas_call x1, Pallas kernels, per_device(): pl.pallas_call(leave, out_shape=(jax.ShapeDtypeStruct((LAT, ROWS), BF16),...  11 us

profile of v3, /device:TPU:1, one launch (start us, length us, event | category | flops | bytes accessed | tf_op | source)
XLA Modules:
  0.0 73.1 jit_solution(1399286966255453257)
XLA Ops:
  0.6 61.2 %shard_map.131 = (bf16[64,192]{1,0:T(8,128)(2,1)}, bf16[192,768]{1,0:T(8,128)(2,1)}) custom-call(bf16[192,3072]{1,0:T(8,128)(2,1)} %pixels.1, bf16[3072,512]{1,0:T(8,128)(2,1)} %w_encode.1, bf16[64,512]{1,0:T(8,128)(2,1)} %bitcast.9, s32[1,192]{1,0:T(1,128)} %bitcast.14, bf16[64,3072]{1,0:T(8,128)(2,1)} %w_embed.1, f32[1,3072]{1,0:T(1,128)} %bitcast.11, ...), custom_call_target="tpu_custom_call" | custom-call | tf_op jit(solution)/shard_map/pallas_call | solution.py:485
  61.9 11.0 %shard_map.132 = (bf16[64,192]{1,0:T(8,128)(2,1)}, bf16[192,768]{1,0:T(8,128)(2,1)}) custom-call(bf16[64,192]{1,0:T(8,128)(2,1)} %get-tuple-element.6.lat_ref, bf16[192,768]{1,0:T(8,128)(2,1)} %get-tuple-element.7.block_ref), custom_call_target="tpu_custom_call" | custom-call | tf_op jit(solution)/shard_map/pallas_call | solution.py:493

commit v4 on v3

--- a/solution.py
+++ b/solution.py
@@ -54,19 +54,22 @@
     x = (s // 8) % 4
     y = (s // 2) % 4
     c = s % 2
-    u = x + c * (y - x)
-    v = y + c * (x - y)
     b = z * 4 + y
-    at = (v * 4 + u) * 2 + z
+    at = z * (x * 4 + y) + (1 - z) * (y * 4 + x)
     sibling = {"sec": s + 1 - 2 * c}
     tp_peers = [{"tp": (t + k) % 4} for k in range(1, 4)]
     x_at = [(x + k) % 4 for k in range(1, 4)]
     x_peers = [{"sec": s + (xx - x) * 8} for xx in x_at]
     b_at = [(b + k) % 8 for k in range(1, 8)]
     b_peers = [{"sec": (bb // 4) * 32 + x * 8 + (bb % 4) * 2 + c} for bb in b_at]
-    z_peer = {"sec": s + (1 - 2 * z) * 32}
-    u_peers = [{"sec": s + ((u + k) % 4 - u) * (8 - 6 * c)} for k in range(1, 4)]
-    v_peers = [{"sec": s + ((v + k) % 4 - v) * (2 + 6 * c)} for k in range(1, 4)]
+    y_peers = [{"sec": s + ((y + k) % 4 - y) * 2} for k in range(1, 4)]
+    cross_x = [{"sec": s + (1 - 2 * z) * 32 + (xx - x) * 8} for xx in x_at]
+    inner = z * y + (1 - z) * x
+    stride = 8 - 6 * z
+    plane_peers = [{"sec": s + ((inner + k) % 4 - inner) * stride} for k in range(1, 4)]
+    plane_peers += [
+        {"sec": s + (1 - 2 * z) * 32 + ((inner + k) % 4 - inner) * stride} for k in range(4)
+    ]
     m_to = {"tp": s // 16, "sec": ((s % 16) * 4 + t + 1) % 64}
     back = (s + 63) % 64
     m_from = {"tp": back % 4, "sec": t * 16 + back // 4}
@@ -84,6 +87,31 @@
         sent.append(copy)
         return copy
 
+    def spread_plane(ref):
+        return [push(ref.at[z, c, at], ref.at[z, c, at], device) for device in plane_peers]
+
+    by_y = pl.ds(y * 4, 4)
+    by_x = pl.ds(x * 4, 4)
+
+    def spread_rest(ref):
+        pairs = []
+        for k in range(3):
+            pairs.append(
+                (
+                    push(ref.at[0, c, by_y], ref.at[0, c, by_y], y_peers[k]),
+                    push(ref.at[1, c, by_x], ref.at[1, c, by_x], x_peers[k]),
+                )
+            )
+        return pairs
+
+    def hand_over(ref, k):
+        from_y = pl.ds(((y + 4 - k) % 4) * 4, 4)
+        from_x = pl.ds(((x + 4 - k) % 4) * 4, 4)
+        return (
+            push(ref.at[0, c, from_y], ref.at[0, c, from_y], sibling),
+            push(ref.at[1, c, from_x], ref.at[1, c, from_x], sibling),
+        )
+
     loads = [0]
 
     def fetch(src, dst):
@@ -103,7 +131,7 @@
     ]
 
     barrier = pltpu.get_barrier_semaphore()
-    greet = tp_peers + [sibling] + x_peers + b_peers + [m_from]
+    greet = tp_peers + [sibling] + x_peers + b_peers + cross_x + [m_from]
     for device in greet:
         pl.semaphore_signal(barrier, inc=1, device_id=device, device_id_type=MESH)
 
@@ -181,8 +209,8 @@
         turn = (ROWS * (1 - c) - LAT * c - LAT * k + 2 * LANES) % LANES
         piece = jnp.where(spare & (row == k), pltpu.roll(high, turn, 1), piece)
         piece = jnp.where(spare & (row == k + 3), pltpu.roll(low, turn, 1), piece)
-    slots[c, at] = piece.astype(BF16)
-    lat_z = push(slots.at[c, at], slots.at[c, at], z_peer)
+    slots[z, c, at] = piece.astype(BF16)
+    lat_plane = spread_plane(slots)
 
     for copy in w_x:
         copy.wait_recv()
@@ -191,10 +219,6 @@
         added += x_in[k].astype(F32)
     y_in[b] = added.astype(BF16)
     w_b = [push(y_in.at[b], y_in.at[b], device) for device in b_peers]
-
-    lat_z.wait_recv()
-    pair = pl.ds((v * 4 + u) * 2, 2)
-    lat_u = [push(slots.at[c, pair], slots.at[c, pair], device) for device in u_peers]
 
     for copy in w_b:
         copy.wait_recv()
@@ -205,23 +229,10 @@
     weights[place, :] = added.astype(BF16)
     w_g = [push(weights.at[place], weights.at[place], device) for device in x_peers]
 
-    for copy in lat_u:
-        copy.wait_recv()
-    group = pl.ds(v * 8, 8)
-    right, left = v_peers[0], v_peers[2]
-
-    def halves(which):
-        return [pl.ds(which * 8, 4), pl.ds(which * 8 + 4, 4)]
-
-    def forward(place, device):
-        return push(slots.at[c, place], slots.at[c, place], device)
-
-    own_a, own_b = halves(v)
-    right_a = forward(own_a, right)
-    left_b = forward(own_b, left)
-    right_b = forward(own_b, right)
-    left_a = forward(own_a, left)
-    lat_c = [forward(group, sibling)]
+    for copy in lat_plane:
+        copy.wait_recv()
+    lat_rest = spread_rest(slots)
+    lat_c = [hand_over(slots, 0)]
 
     for copy in w_g:
         copy.wait_recv()
@@ -246,8 +257,8 @@
             n = 4 * k + i
             lats, scales = [], []
             for zz in range(2):
-                near = slots[0, g0 * 8 + 2 * i + zz]
-                far = slots[1, g1 * 8 + 2 * i + zz]
+                near = slots[zz, 0, (g1 if zz else g0) * 4 + i]
+                far = slots[zz, 1, (g1 if zz else g0) * 4 + i]
                 middle = jnp.where(lane_t < LAT, near[:, HD:].astype(F32), far[:, :HD].astype(F32))
                 lats += [near[:, :HD].astype(F32), middle, far[:, HD:].astype(F32)]
                 sl = near[0:16, HD:].astype(F32)
@@ -264,11 +275,8 @@
             lat_c32 = jnp.concatenate(lats, axis=1)
             scale_row = jnp.concatenate(scales, axis=1)
             lat_cb = lat_c32.astype(BF16)
-            upper = lane_c // 384
-            inner = lane_c - upper * 384
-            base0 = i * 8 * ROWS + g0 * 2 * ROWS
-            base1 = g1 * 8 * ROWS + i * 2 * ROWS + ROWS
-            token = inner + upper * (32 * ROWS) + jnp.where(inner < ROWS, base0, base1 - ROWS)
+            start = jnp.where(lane_c < 384, (i * 8 + g0 * 2) * ROWS, (32 + g1 * 8 + i * 2) * ROWS - 384)
+            token = lane_c + start
             hit = jnp.where(origin == token, 1.0, 0.0).astype(BF16)
             latq[0:ROWS, 0:LAT] += dot(hit, lat_cb, NT)
             scaled = lat_c32 * scale_row
@@ -288,29 +296,17 @@
                 keys[h, n, 0:LAT, :] = (scaled * inv).astype(BF16)
                 keys[h, n, LAT:FEAT, :] = tail.astype(BF16)
 
-    for k, turn in enumerate((0, 1, 3, 2)):
-        came = (v + 4 - turn) % 4
-        if turn == 1:
-            right_a.wait_recv()
-            relay_a = forward(halves(came)[0], right)
-            left_b.wait_recv()
-            relay_b = forward(halves((v + 1) % 4)[1], left)
-            right_b.wait_recv()
-        elif turn == 3:
-            left_a.wait_recv()
-        elif turn == 2:
-            relay_a.wait_recv()
-            relay_b.wait_recv()
+    for k in range(4):
         if k:
-            lat_c.append(forward(pl.ds(came * 8, 8), sibling))
-        lat_c[k].wait_recv()
-        prepare(k, (y + 4 - turn) % 4, (x + 4 - turn) % 4)
-        if k == 1:
-            m_move.wait_recv()
-            m_slots[c, at] = m_in[1]
-            m_z = push(m_slots.at[c, at], m_slots.at[c, at], z_peer)
-    m_z.wait_recv()
-    m_u = [push(m_slots.at[c, pair], m_slots.at[c, pair], device) for device in u_peers]
+            for copy in lat_rest[k - 1]:
+                copy.wait_recv()
+            lat_c.append(hand_over(slots, k))
+        for copy in lat_c[k]:
+            copy.wait_recv()
+        prepare(k, (y + 4 - k) % 4, (x + 4 - k) % 4)
+    m_move.wait_recv()
+    m_slots[z, c, at] = m_in[1]
+    m_plane = spread_plane(m_slots)
 
     rows = latq[0:ROWS, :].astype(BF16)
     lat_out[...] = latq[...].T[0:LAT, 0:ROWS].astype(BF16)
@@ -357,10 +353,6 @@
     for n in range(CHUNKS):
         most = score(n, 0, most)
     running[0] = most
-    for copy in m_u:
-        copy.wait_recv()
-    m_v = [push(m_slots.at[c, group], m_slots.at[c, group], device) for device in v_peers]
-    m_c = [push(m_slots.at[c, group], m_slots.at[c, group], sibling)]
     mixed = []
     for h in range(HEADS):
         top[h] = jnp.broadcast_to(jnp.max(running[h], axis=1, keepdims=True), (ROWS, HD))
@@ -377,25 +369,29 @@
         if h + 1 < HEADS:
             running[h + 1] = following
         mixed.append(accum[h] / accum[h, :, LAT : LAT + 1])
+        if h == 0:
+            for copy in m_plane:
+                copy.wait_recv()
+            m_rest = spread_rest(m_slots)
         if h == 1:
             first[t] = jnp.where(lane_q < LAT, mixed[0], pltpu.roll(mixed[1], LAT, 1)).astype(BF16)
             o_first = [push(first.at[t], first.at[t], device) for device in tp_peers]
-            for k in range(1, 4):
-                m_v[k - 1].wait_recv()
-                came = pl.ds(((v + 4 - k) % 4) * 8, 8)
-                m_c.append(push(m_slots.at[c, came], m_slots.at[c, came], sibling))
     lower = pltpu.roll(mixed[2][ROWS // 2 :, :], LAT, 1)
     second[t] = jnp.where(lane_q[0 : ROWS // 2] < LAT, mixed[2][0 : ROWS // 2, :], lower).astype(BF16)
     o_second = [push(second.at[t], second.at[t], device) for device in tp_peers]
 
+    m_c = list(hand_over(m_slots, 0))
+    for k in range(1, 4):
+        for copy in m_rest[k - 1]:
+            copy.wait_recv()
+        m_c += hand_over(m_slots, k)
     for copy in m_c:
         copy.wait_recv()
     for slot in range(64):
-        cc, rest = slot // 32, slot % 32
-        vv, uu, zz = rest // 8, (rest // 2) % 4, rest % 2
-        xx, yy = (uu, vv) if cc == 0 else (vv, uu)
+        zz, cc, outer, step = slot // 32, (slot // 16) % 2, (slot // 4) % 4, slot % 4
+        xx, yy = (outer, step) if zz else (step, outer)
         origin_at = (zz * 32 + xx * 8 + yy * 2 + cc + 63) % 64
-        assembled[origin_at % 4, pl.ds((origin_at // 4) * MCOLS, MCOLS), :] = m_slots[cc, rest]
+        assembled[origin_at % 4, pl.ds((origin_at // 4) * MCOLS, MCOLS), :] = m_slots[zz, cc, outer * 4 + step]
     quarter = pl.ds(pl.multiple_of(t * QUARTER, QUARTER), QUARTER)
     embedded = dot(rows[:, 0:LAT], emb_v[:, quarter], NN)
     for copy in o_first:
@@ -416,18 +412,12 @@
         copy.wait_send()
 
 
-def leave(lat_ref, block_ref, lat_to, block_to, sem):
-    copies = [
-        pltpu.make_async_copy(lat_ref, lat_to, sem.at[0]),
-        pltpu.make_async_copy(block_ref, block_to, sem.at[1]),
-    ]
-    for copy in copies:
-        copy.start()
-    for copy in copies:
-        copy.wait()
-
-
-COPIES = 50
+def leave(lat_ref, block_ref, lat_to, block_to):
+    lat_to[...] = lat_ref[...]
+    block_to[...] = block_ref[...]
+
+
+COPIES = 67
 LOADS = 18
 
 
@@ -462,9 +452,9 @@
         vmem((4, 144, HD), BF16),
         vmem((8, 144, HD), BF16),
         vmem((3 * WID, HD), BF16),
-        vmem((2, 32, LAT, LANES), BF16),
+        vmem((2, 2, 16, LAT, LANES), BF16),
         vmem((2, MCOLS, LANES), BF16),
-        vmem((2, 32, MCOLS, LANES), BF16),
+        vmem((2, 2, 16, MCOLS, LANES), BF16),
         vmem((LANES, HD), F32),
         vmem((HD, LANES), F32),
         vmem((HEADS, ROWS, HD), BF16),
@@ -493,9 +483,6 @@
     lat, out = pl.pallas_call(
         leave,
         out_shape=(jax.ShapeDtypeStruct((LAT, ROWS), BF16), jax.ShapeDtypeStruct((ROWS, QUARTER), BF16)),
-        in_specs=[pl.BlockSpec(memory_space=pl.ANY)] * 2,
-        out_specs=(pl.BlockSpec(memory_space=pl.ANY), pl.BlockSpec(memory_space=pl.ANY)),
-        scratch_shapes=[pltpu.SemaphoreType.DMA((2,))],
     )(lat, out)
     return lat.T, out
 

time: 73.1 us -> 67.1 us (0.918)
  Pallas kernels: 72.3 us -> 66.4 us
    pallas_call x1, Pallas kernels: 11 us -> 1.72 us  [per_device(): pl.pallas_call(leave, out_shape=(jax.ShapeDtypeStruct((LAT, ROWS), BF16),...]
    pallas_call x1, Pallas kernels: 61.2 us -> 64.7 us  [per_device(): pl.pallas_call(kernel, out_shape=(jax.ShapeDtypeStruct((LAT, ROWS), BF16)...]
where the time goes in v4:
time: 67.1 us; the launch traced here: 67 us
  Pallas kernels  66.4 us (99%)
    pallas_call x1, Pallas kernels, per_device(): pl.pallas_call(kernel, out_shape=(jax.ShapeDtypeStruct((LAT, ROWS), BF16)...  64.7 us
    pallas_call x1, Pallas kernels, per_device(): pl.pallas_call(leave, out_shape=(jax.ShapeDtypeStruct((LAT, ROWS), BF16),...  1.72 us

profile of v4, /device:TPU:1, one launch (start us, length us, event | category | flops | bytes accessed | tf_op | source)
XLA Modules:
  0.0 67.0 jit_solution(5598995963676013841)
XLA Ops:
  0.6 64.7 %shard_map.131 = (bf16[64,192]{1,0:T(8,128)(2,1)}, bf16[192,768]{1,0:T(8,128)(2,1)}) custom-call(bf16[192,3072]{1,0:T(8,128)(2,1)} %pixels.1, bf16[3072,512]{1,0:T(8,128)(2,1)} %w_encode.1, bf16[64,512]{1,0:T(8,128)(2,1)} %bitcast.9, s32[1,192]{1,0:T(1,128)} %bitcast.14, bf16[64,3072]{1,0:T(8,128)(2,1)} %w_embed.1, f32[1,3072]{1,0:T(1,128)} %bitcast.11, ...), custom_call_target="tpu_custom_call" | custom-call | tf_op jit(solution)/shard_map/pallas_call | solution.py:475
  65.3 1.7 %shard_map.132 = (bf16[64,192]{1,0:T(8,128)(2,1)}, bf16[192,768]{1,0:T(8,128)(2,1)}) custom-call(bf16[64,192]{1,0:T(8,128)(2,1)} %get-tuple-element.6.lat_ref, bf16[192,768]{1,0:T(8,128)(2,1)} %get-tuple-element.7.block_ref), custom_call_target="tpu_custom_call" | custom-call | tf_op jit(solution)/shard_map/pallas_call | solution.py:483

commit v5 on v4

--- a/solution.py
+++ b/solution.py
@@ -43,7 +43,7 @@
     pixels, w_encode, w_latent, source, w_embed, mod_shift, mod_scale, gate, q_gain, k_gain, w_qkv, w_out,
     lat_out, block_out,
     pix_v, enc_v, wlat_v, src_v, emb_v, shift_v, scale_v, gate_v, qg_v, kg_v, wqkv_v, wout_v,
-    wide, centred, centred_t, wp, lat_in, core_in, half, x_in, y_in, weights,
+    wide, centred, centred_t, wp, lat_in, x_in, y_in, weights,
     slots, m_in, m_slots, latq, square, queries, keys, vals, s_even, s_odd, running, top, accum,
     first, second, assembled,
     load, send, recv,
@@ -70,9 +70,10 @@
     plane_peers += [
         {"sec": s + (1 - 2 * z) * 32 + ((inner + k) % 4 - inner) * stride} for k in range(4)
     ]
-    m_to = {"tp": s // 16, "sec": ((s % 16) * 4 + t + 1) % 64}
-    back = (s + 63) % 64
-    m_from = {"tp": back % 4, "sec": t * 16 + back // 4}
+    m_peer = {"tp": s // 16, "sec": (t // 2) * 32 + (2 * (t % 2) + x % 2) * 8 + y * 2 + 1 - c}
+    a = x * 2 + c
+    a_at = [(a + k) % 8 for k in range(1, 8)]
+    a_peers = [{"sec": z * 32 + (aa // 2) * 8 + y * 2 + aa % 2} for aa in a_at]
 
     sent = []
     used = [0]
@@ -112,6 +113,11 @@
             push(ref.at[1, c, from_x], ref.at[1, c, from_x], sibling),
         )
 
+    barrier = pltpu.get_barrier_semaphore()
+    greet = [m_peer] + tp_peers + b_peers + cross_x + a_peers
+    for device in greet:
+        pl.semaphore_signal(barrier, inc=1, device_id=device, device_id_type=MESH)
+
     loads = [0]
 
     def fetch(src, dst):
@@ -129,11 +135,6 @@
     late = [
         fetch(source, src_v), fetch(gate, gate_v), fetch(q_gain, qg_v), fetch(k_gain, kg_v), fetch(w_out, wout_v)
     ]
-
-    barrier = pltpu.get_barrier_semaphore()
-    greet = tp_peers + [sibling] + x_peers + b_peers + cross_x + [m_from]
-    for device in greet:
-        pl.semaphore_signal(barrier, inc=1, device_id=device, device_id_type=MESH)
 
     for copy in early:
         copy.wait()
@@ -151,6 +152,11 @@
     for i in range(3):
         wp[i * WID : (i + 1) * WID, :] = (dot(wqkv_v[i], high, TN) + dot(wqkv_v[i], low, TN)).astype(BF16)
 
+    high, low = split(emb_v[...].astype(F32) - mean)
+    both_terms = jnp.concatenate([high, low], axis=0)
+    centred[...] = both_terms.astype(BF16)
+    centred_t[...] = both_terms.T.astype(BF16)
+
     total = jnp.zeros((ROWS, 512), F32)
     for k in range(PARTS):
         parts[k][0].wait()
@@ -162,30 +168,28 @@
     wide[0:LAT, 0:ROWS] = dot(wlat_v[...], hidden, NT)
     lat_in[t] = pltpu.roll(wide[0:LAT, :], LAT * c, 1).astype(BF16)
 
-    pl.semaphore_wait(barrier, len(greet))
-    mine = pl.ds(pl.multiple_of(c * 576, 576), 576)
-    other = pl.ds(pl.multiple_of((1 - c) * 576, 576), 576)
-    w_core = push(wp.at[other], core_in, sibling)
-    lat_tp = [push(lat_in.at[t], lat_in.at[t], device) for device in tp_peers]
-
-    high, low = split(emb_v[...].astype(F32) - mean)
-    both_terms = jnp.concatenate([high, low], axis=0)
-    centred[...] = both_terms.astype(BF16)
-    centred_t[...] = both_terms.T.astype(BF16)
-
-    w_core.wait_recv()
-    half[...] = (wp[mine, :].astype(F32) + core_in[...].astype(F32)).astype(BF16)
-    w_x = []
-    for k in range(3):
-        w_x.append(push(half.at[pl.ds(pl.multiple_of(x_at[k] * 144, 144), 144)], x_in.at[x], x_peers[k]))
-    x_in[x] = half[pl.ds(pl.multiple_of(x * 144, 144), 144), :]
-
     for copy in late:
         copy.wait()
     square[...] = jnp.zeros_like(square)
     square[:, 0:ROWS] = jnp.broadcast_to(src_v[...].astype(F32), (HD, ROWS))
     origin = square[...].T[0:ROWS, 0:1].astype(jnp.int32)
     latq[...] = jnp.zeros_like(latq)
+    place = pl.ds(pl.multiple_of(a * 144, 144), 144)
+
+    pl.semaphore_wait(barrier, len(greet))
+    lat_tp = [push(lat_in.at[t], lat_in.at[t], device) for device in tp_peers]
+
+    w_x = []
+    for k in range(7):
+        w_x.append(push(wp.at[pl.ds(pl.multiple_of(a_at[k] * 144, 144), 144)], x_in.at[a], a_peers[k]))
+    x_in[a] = wp[place, :]
+    for copy in w_x:
+        copy.wait_recv()
+    added = x_in[0].astype(F32)
+    for k in range(1, 8):
+        added += x_in[k].astype(F32)
+    y_in[b] = added.astype(BF16)
+    w_b = [push(y_in.at[b], y_in.at[b], device) for device in b_peers]
 
     for copy in lat_tp:
         copy.wait_recv()
@@ -212,22 +216,13 @@
     slots[z, c, at] = piece.astype(BF16)
     lat_plane = spread_plane(slots)
 
-    for copy in w_x:
-        copy.wait_recv()
-    added = x_in[0].astype(F32)
-    for k in range(1, 4):
-        added += x_in[k].astype(F32)
-    y_in[b] = added.astype(BF16)
-    w_b = [push(y_in.at[b], y_in.at[b], device) for device in b_peers]
-
     for copy in w_b:
         copy.wait_recv()
     added = y_in[0].astype(F32)
     for k in range(1, 8):
         added += y_in[k].astype(F32)
-    place = pl.ds(pl.multiple_of(c * 576 + x * 144, 144), 144)
     weights[place, :] = added.astype(BF16)
-    w_g = [push(weights.at[place], weights.at[place], device) for device in x_peers]
+    w_g = [push(weights.at[place], weights.at[place], device) for device in a_peers]
 
     for copy in lat_plane:
         copy.wait_recv()
@@ -236,8 +231,6 @@
 
     for copy in w_g:
         copy.wait_recv()
-    w_last = push(weights.at[mine], weights.at[mine], sibling)
-    w_last.wait_recv()
 
     wide_m = lax.broadcasted_iota(jnp.int32, (MCOLS, HD), 1)
     terms = [
@@ -246,7 +239,7 @@
     ]
     m_in[0, :, 0:HD] = jnp.where(wide_m < LAT, terms[0], pltpu.roll(terms[1], LAT, 1)).astype(BF16)
     m_in[0, :, HD:LANES] = jnp.where(wide_m < LAT, terms[2], terms[0] + terms[1] + terms[2]).astype(BF16)
-    m_move = push(m_in.at[0], m_in.at[1], m_to)
+    m_move = push(m_in.at[0], m_in.at[1], m_peer)
 
     lane_t = lax.broadcasted_iota(jnp.int32, (1, HD), 1)
     lane_c = lax.broadcasted_iota(jnp.int32, (1, CHUNK), 1)
@@ -297,16 +290,18 @@
                 keys[h, n, LAT:FEAT, :] = tail.astype(BF16)
 
     for k in range(4):
-        if k:
-            for copy in lat_rest[k - 1]:
-                copy.wait_recv()
-            lat_c.append(hand_over(slots, k))
         for copy in lat_c[k]:
             copy.wait_recv()
         prepare(k, (y + 4 - k) % 4, (x + 4 - k) % 4)
-    m_move.wait_recv()
-    m_slots[z, c, at] = m_in[1]
-    m_plane = spread_plane(m_slots)
+        if k == 0:
+            for j in range(1, 4):
+                for copy in lat_rest[j - 1]:
+                    copy.wait_recv()
+                lat_c.append(hand_over(slots, j))
+        if k == 2:
+            m_move.wait_recv()
+            m_slots[z, c, at] = m_in[1]
+            m_plane = spread_plane(m_slots)
 
     rows = latq[0:ROWS, :].astype(BF16)
     lat_out[...] = latq[...].T[0:LAT, 0:ROWS].astype(BF16)
@@ -362,6 +357,10 @@
         if h + 1 < HEADS:
             following = running[h + 1]
         for n in range(CHUNKS):
+            if h == 0 and n == CHUNKS // 2:
+                for copy in m_plane:
+                    copy.wait_recv()
+                m_rest = spread_rest(m_slots)
             if h + 1 < HEADS:
                 following = score(n, h + 1, following)
             added += weigh(n, h, most)
@@ -369,10 +368,6 @@
         if h + 1 < HEADS:
             running[h + 1] = following
         mixed.append(accum[h] / accum[h, :, LAT : LAT + 1])
-        if h == 0:
-            for copy in m_plane:
-                copy.wait_recv()
-            m_rest = spread_rest(m_slots)
         if h == 1:
             first[t] = jnp.where(lane_q < LAT, mixed[0], pltpu.roll(mixed[1], LAT, 1)).astype(BF16)
             o_first = [push(first.at[t], first.at[t], device) for device in tp_peers]
@@ -390,8 +385,8 @@
     for slot in range(64):
         zz, cc, outer, step = slot // 32, (slot // 16) % 2, (slot // 4) % 4, slot % 4
         xx, yy = (outer, step) if zz else (step, outer)
-        origin_at = (zz * 32 + xx * 8 + yy * 2 + cc + 63) % 64
-        assembled[origin_at % 4, pl.ds((origin_at // 4) * MCOLS, MCOLS), :] = m_slots[zz, cc, outer * 4 + step]
+        source_tp, column = 2 * zz + xx // 2, ((xx % 2) * 8 + yy * 2 + 1 - cc) * MCOLS
+        assembled[source_tp, pl.ds(column, MCOLS), :] = m_slots[zz, cc, outer * 4 + step]
     quarter = pl.ds(pl.multiple_of(t * QUARTER, QUARTER), QUARTER)
     embedded = dot(rows[:, 0:LAT], emb_v[:, quarter], NN)
     for copy in o_first:
@@ -417,7 +412,7 @@
     block_to[...] = block_ref[...]
 
 
-COPIES = 67
+COPIES = 73
 LOADS = 18
 
 
@@ -447,9 +442,7 @@
         vmem((DIM, HD), BF16),
         vmem((3 * WID, HD), BF16),
         vmem((4, LAT, LANES), BF16),
-        vmem((576, HD), BF16),
-        vmem((576, HD), BF16),
-        vmem((4, 144, HD), BF16),
+        vmem((8, 144, HD), BF16),
         vmem((8, 144, HD), BF16),
         vmem((3 * WID, HD), BF16),
         vmem((2, 2, 16, LAT, LANES), BF16),

time: 67.1 us -> 63.1 us (0.940)
  Pallas kernels: 66.4 us -> 62.3 us
    pallas_call x1, Pallas kernels: 64.7 us -> 60.6 us  [per_device(): pl.pallas_call(kernel, out_shape=(jax.ShapeDtypeStruct((LAT, ROWS), BF16)...]
where the time goes in v5:
time: 63.1 us; the launch traced here: 63 us
  Pallas kernels  62.3 us (99%)
  between operations  0.64 us (1%)
    pallas_call x1, Pallas kernels, per_device(): pl.pallas_call(kernel, out_shape=(jax.ShapeDtypeStruct((LAT, ROWS), BF16)...  60.6 us
    pallas_call x1, Pallas kernels, per_device(): pl.pallas_call(leave, out_shape=(jax.ShapeDtypeStruct((LAT, ROWS), BF16),...  1.72 us

profile of v5, /device:TPU:1, one launch (start us, length us, event | category | flops | bytes accessed | tf_op | source)
XLA Modules:
  0.0 63.0 jit_solution(3844726277423872594)
XLA Ops:
  0.6 60.6 %shard_map.131 = (bf16[64,192]{1,0:T(8,128)(2,1)}, bf16[192,768]{1,0:T(8,128)(2,1)}) custom-call(bf16[192,3072]{1,0:T(8,128)(2,1)} %pixels.1, bf16[3072,512]{1,0:T(8,128)(2,1)} %w_encode.1, bf16[64,512]{1,0:T(8,128)(2,1)} %bitcast.9, s32[1,192]{1,0:T(1,128)} %bitcast.14, bf16[64,3072]{1,0:T(8,128)(2,1)} %w_embed.1, f32[1,3072]{1,0:T(1,128)} %bitcast.11, ...), custom_call_target="tpu_custom_call" | custom-call | tf_op jit(solution)/shard_map/pallas_call | solution.py:468
  61.3 1.7 %shard_map.132 = (bf16[64,192]{1,0:T(8,128)(2,1)}, bf16[192,768]{1,0:T(8,128)(2,1)}) custom-call(bf16[64,192]{1,0:T(8,128)(2,1)} %get-tuple-element.6.lat_ref, bf16[192,768]{1,0:T(8,128)(2,1)} %get-tuple-element.7.block_ref), custom_call_target="tpu_custom_call" | custom-call | tf_op jit(solution)/shard_map/pallas_call | solution.py:476

commit v6 on v5

--- a/solution.py
+++ b/solution.py
@@ -45,7 +45,7 @@
     pix_v, enc_v, wlat_v, src_v, emb_v, shift_v, scale_v, gate_v, qg_v, kg_v, wqkv_v, wout_v,
     wide, centred, centred_t, wp, lat_in, x_in, y_in, weights,
     slots, m_in, m_slots, latq, square, queries, keys, vals, s_even, s_odd, running, top, accum,
-    first, second, assembled,
+    packed, assembled,
     load, send, recv,
 ):
     s = lax.axis_index("sec")
@@ -298,7 +298,7 @@
                 for copy in lat_rest[j - 1]:
                     copy.wait_recv()
                 lat_c.append(hand_over(slots, j))
-        if k == 2:
+        if k == 1:
             m_move.wait_recv()
             m_slots[z, c, at] = m_in[1]
             m_plane = spread_plane(m_slots)
@@ -348,7 +348,7 @@
     for n in range(CHUNKS):
         most = score(n, 0, most)
     running[0] = most
-    mixed = []
+    o_heads = []
     for h in range(HEADS):
         top[h] = jnp.broadcast_to(jnp.max(running[h], axis=1, keepdims=True), (ROWS, HD))
 
@@ -357,29 +357,27 @@
         if h + 1 < HEADS:
             following = running[h + 1]
         for n in range(CHUNKS):
-            if h == 0 and n == CHUNKS // 2:
+            if h == 0 and n == 4:
                 for copy in m_plane:
                     copy.wait_recv()
                 m_rest = spread_rest(m_slots)
+                m_c = list(hand_over(m_slots, 0))
+            if h == 2 and n == CHUNKS // 2:
+                for j in range(1, 4):
+                    for copy in m_rest[j - 1]:
+                        copy.wait_recv()
+                    m_c += hand_over(m_slots, j)
             if h + 1 < HEADS:
                 following = score(n, h + 1, following)
             added += weigh(n, h, most)
         accum[h, :, 0:FEAT] = added
         if h + 1 < HEADS:
             running[h + 1] = following
-        mixed.append(accum[h] / accum[h, :, LAT : LAT + 1])
-        if h == 1:
-            first[t] = jnp.where(lane_q < LAT, mixed[0], pltpu.roll(mixed[1], LAT, 1)).astype(BF16)
-            o_first = [push(first.at[t], first.at[t], device) for device in tp_peers]
-    lower = pltpu.roll(mixed[2][ROWS // 2 :, :], LAT, 1)
-    second[t] = jnp.where(lane_q[0 : ROWS // 2] < LAT, mixed[2][0 : ROWS // 2, :], lower).astype(BF16)
-    o_second = [push(second.at[t], second.at[t], device) for device in tp_peers]
-
-    m_c = list(hand_over(m_slots, 0))
-    for k in range(1, 4):
-        for copy in m_rest[k - 1]:
-            copy.wait_recv()
-        m_c += hand_over(m_slots, k)
+        mixed = accum[h] / accum[h, :, LAT : LAT + 1]
+        lower = pltpu.roll(mixed[ROWS // 2 :, :], LAT, 1)
+        packed[h, t] = jnp.where(lane_q[0 : ROWS // 2] < LAT, mixed[0 : ROWS // 2, :], lower).astype(BF16)
+        o_heads.append([push(packed.at[h, t], packed.at[h, t], device) for device in tp_peers])
+
     for copy in m_c:
         copy.wait_recv()
     for slot in range(64):
@@ -389,18 +387,22 @@
         assembled[source_tp, pl.ds(column, MCOLS), :] = m_slots[zz, cc, outer * 4 + step]
     quarter = pl.ds(pl.multiple_of(t * QUARTER, QUARTER), QUARTER)
     embedded = dot(rows[:, 0:LAT], emb_v[:, quarter], NN)
-    for copy in o_first:
-        copy.wait_recv()
-    total = dot(first[0], assembled[0, :, 0:HD], NT)
-    for k in range(1, 4):
-        total += dot(first[k], assembled[k, :, 0:HD], NT)
-    for copy in o_second:
-        copy.wait_recv()
     one = jnp.where(lane_q == LAT, 1.0, 0.0)
+
+    def unpacked(h, k):
+        both = packed[h, k].astype(F32)
+        return jnp.concatenate([both, pltpu.roll(both, LAT, 1)], axis=0)
+
+    for copy in o_heads[0] + o_heads[1]:
+        copy.wait_recv()
+    total = jnp.zeros((ROWS, QUARTER), F32)
     for k in range(4):
-        packed = second[k].astype(F32)
-        whole = jnp.concatenate([packed, pltpu.roll(packed, LAT, 1)], axis=0)
-        whole = jnp.where(lane_q < LAT, whole, one).astype(BF16)
+        whole = jnp.where(lane_q < LAT, unpacked(0, k), pltpu.roll(unpacked(1, k), LAT, 1)).astype(BF16)
+        total += dot(whole, assembled[k, :, 0:HD], NT)
+    for copy in o_heads[2]:
+        copy.wait_recv()
+    for k in range(4):
+        whole = jnp.where(lane_q < LAT, unpacked(2, k), one).astype(BF16)
         total += dot(whole, assembled[k, :, HD:LANES], NT)
     block_out[...] = (embedded + gate_v[:, quarter] * total).astype(BF16)
     for copy in sent:
@@ -412,7 +414,7 @@
     block_to[...] = block_ref[...]
 
 
-COPIES = 73
+COPIES = 76
 LOADS = 18
 
 
@@ -458,8 +460,7 @@
         vmem((HEADS, ROWS, HD), F32),
         vmem((HEADS, ROWS, HD), F32),
         vmem((HEADS, ROWS, HD), F32),
-        vmem((4, ROWS, HD), BF16),
-        vmem((4, ROWS // 2, HD), BF16),
+        vmem((HEADS, 4, ROWS // 2, HD), BF16),
         vmem((4, QUARTER, LANES), BF16),
         pltpu.SemaphoreType.DMA((LOADS,)),
         pltpu.SemaphoreType.DMA((COPIES,)),

time: 63.1 us -> 59.6 us (0.945)
  Pallas kernels: 62.3 us -> 58.8 us
    pallas_call x1, Pallas kernels: 60.6 us -> 57.1 us  [per_device(): pl.pallas_call(kernel, out_shape=(jax.ShapeDtypeStruct((LAT, ROWS), BF16)...]
where the time goes in v6:
time: 59.6 us; the launch traced here: 59.5 us
  Pallas kernels  58.8 us (99%)
  between operations  0.64 us (1%)
    pallas_call x1, Pallas kernels, per_device(): pl.pallas_call(kernel, out_shape=(jax.ShapeDtypeStruct((LAT, ROWS), BF16)...  57.1 us
    pallas_call x1, Pallas kernels, per_device(): pl.pallas_call(leave, out_shape=(jax.ShapeDtypeStruct((LAT, ROWS), BF16),...  1.72 us

profile of v6, /device:TPU:1, one launch (start us, length us, event | category | flops | bytes accessed | tf_op | source)
XLA Modules:
  0.0 59.5 jit_solution(16195078053039303442)
XLA Ops:
  0.6 57.1 %shard_map.131 = (bf16[64,192]{1,0:T(8,128)(2,1)}, bf16[192,768]{1,0:T(8,128)(2,1)}) custom-call(bf16[192,3072]{1,0:T(8,128)(2,1)} %pixels.1, bf16[3072,512]{1,0:T(8,128)(2,1)} %w_encode.1, bf16[64,512]{1,0:T(8,128)(2,1)} %bitcast.9, s32[1,192]{1,0:T(1,128)} %bitcast.14, bf16[64,3072]{1,0:T(8,128)(2,1)} %w_embed.1, f32[1,3072]{1,0:T(1,128)} %bitcast.11, ...), custom_call_target="tpu_custom_call" | custom-call | tf_op jit(solution)/shard_map/pallas_call | solution.py:469
  57.8 1.7 %shard_map.132 = (bf16[64,192]{1,0:T(8,128)(2,1)}, bf16[192,768]{1,0:T(8,128)(2,1)}) custom-call(bf16[64,192]{1,0:T(8,128)(2,1)} %get-tuple-element.6.lat_ref, bf16[192,768]{1,0:T(8,128)(2,1)} %get-tuple-element.7.block_ref), custom_call_target="tpu_custom_call" | custom-call | tf_op jit(solution)/shard_map/pallas_call | solution.py:477

commit v7 on v6

--- a/solution.py
+++ b/solution.py
@@ -26,6 +26,8 @@
 NN = (((1,), (0,)), ((), ()))
 TN = (((0,), (0,)), ((), ()))
 EPS = 1e-6
+WPACK = 640
+SHARE = WPACK // 8
 LOG2E = 1.4426950408889634
 VMEM_LIMIT = 58 * 1024 * 1024
 
@@ -43,7 +45,7 @@
     pixels, w_encode, w_latent, source, w_embed, mod_shift, mod_scale, gate, q_gain, k_gain, w_qkv, w_out,
     lat_out, block_out,
     pix_v, enc_v, wlat_v, src_v, emb_v, shift_v, scale_v, gate_v, qg_v, kg_v, wqkv_v, wout_v,
-    wide, centred, centred_t, wp, lat_in, x_in, y_in, weights,
+    wide, centred, centred_t, wp, lat_in, x_in, y_in, wsum, weights,
     slots, m_in, m_slots, latq, square, queries, keys, vals, s_even, s_odd, running, top, accum,
     packed, assembled,
     load, send, recv,
@@ -146,11 +148,23 @@
         lax.broadcasted_iota(jnp.int32, (LAT, LANES), 0) < 2, jnp.broadcast_to(shift_v[:, base], (LAT, LANES)), 0.0
     )
     offset = s * MCOLS - block * HD
-    turned = pltpu.roll(wide[...], (LANES - offset) % LANES, 1)[:, 0:HD].T
-    high, low = split(turned[0:MCOLS, :])
+    rolled = pltpu.roll(wide[...], (LANES - offset) % LANES, 1)[:, 0:HD]
+    high, low = split(rolled.T[0:MCOLS, :])
     high, low = high.astype(BF16), low.astype(BF16)
+    shift_high, shift_low = split(rolled[LAT : LAT + 16, 0:MCOLS])
+    shift_high, shift_low = shift_high.astype(BF16), shift_low.astype(BF16)
+    lane_p = lax.broadcasted_iota(jnp.int32, (ROWS, HD), 1)
+    row_p = lax.broadcasted_iota(jnp.int32, (LAT, HD), 0)
+    biases = jnp.zeros((LAT, HD), F32)
     for i in range(3):
-        wp[i * WID : (i + 1) * WID, :] = (dot(wqkv_v[i], high, TN) + dot(wqkv_v[i], low, TN)).astype(BF16)
+        part = dot(wqkv_v[i], high, TN) + dot(wqkv_v[i], low, TN)
+        wp[i * ROWS : (i + 1) * ROWS, :] = jnp.where(
+            lane_p < LAT, part[0:ROWS, :], pltpu.roll(part[ROWS:WID, :], LAT, 1)
+        ).astype(BF16)
+        bias = dot(shift_high, wqkv_v[i], NN) + dot(shift_low, wqkv_v[i], NN)
+        for j in range(HEADS):
+            biases = jnp.where(row_p == HEADS * i + j, bias[0:1, j * HD : (j + 1) * HD], biases)
+    wp[WPACK - LAT : WPACK, :] = biases.astype(BF16)
 
     high, low = split(emb_v[...].astype(F32) - mean)
     both_terms = jnp.concatenate([high, low], axis=0)
@@ -174,14 +188,14 @@
     square[:, 0:ROWS] = jnp.broadcast_to(src_v[...].astype(F32), (HD, ROWS))
     origin = square[...].T[0:ROWS, 0:1].astype(jnp.int32)
     latq[...] = jnp.zeros_like(latq)
-    place = pl.ds(pl.multiple_of(a * 144, 144), 144)
+    place = pl.ds(pl.multiple_of(a * SHARE, SHARE), SHARE)
 
     pl.semaphore_wait(barrier, len(greet))
     lat_tp = [push(lat_in.at[t], lat_in.at[t], device) for device in tp_peers]
 
     w_x = []
     for k in range(7):
-        w_x.append(push(wp.at[pl.ds(pl.multiple_of(a_at[k] * 144, 144), 144)], x_in.at[a], a_peers[k]))
+        w_x.append(push(wp.at[pl.ds(pl.multiple_of(a_at[k] * SHARE, SHARE), SHARE)], x_in.at[a], a_peers[k]))
     x_in[a] = wp[place, :]
     for copy in w_x:
         copy.wait_recv()
@@ -221,8 +235,8 @@
     added = y_in[0].astype(F32)
     for k in range(1, 8):
         added += y_in[k].astype(F32)
-    weights[place, :] = added.astype(BF16)
-    w_g = [push(weights.at[place], weights.at[place], device) for device in a_peers]
+    wsum[place, :] = added.astype(BF16)
+    w_g = [push(wsum.at[place], wsum.at[place], device) for device in a_peers]
 
     for copy in lat_plane:
         copy.wait_recv()
@@ -231,6 +245,15 @@
 
     for copy in w_g:
         copy.wait_recv()
+    biases = jnp.concatenate([wsum[WPACK - LAT : WPACK, :].astype(F32), jnp.zeros((HD - LAT, HD), F32)], axis=0).T
+    lane_w = lax.broadcasted_iota(jnp.int32, (HD, HD), 1)
+    for i in range(3):
+        packed_rows = wsum[i * ROWS : (i + 1) * ROWS, :].astype(F32)
+        both = jnp.concatenate([packed_rows, pltpu.roll(packed_rows, LAT, 1)], axis=0)
+        for j in range(HEADS):
+            n = HEADS * i + j
+            side = jnp.where(lane_w < LAT + 2, biases[:, n : n + 1], 0.0)
+            weights[n * HD : (n + 1) * HD, :] = jnp.where(lane_w < LAT, both[j * HD : (j + 1) * HD, :], side).astype(BF16)
 
     wide_m = lax.broadcasted_iota(jnp.int32, (MCOLS, HD), 1)
     terms = [
@@ -442,10 +465,11 @@
         vmem((HD, LANES), F32),
         vmem((HD, DIM), BF16),
         vmem((DIM, HD), BF16),
-        vmem((3 * WID, HD), BF16),
+        vmem((WPACK, HD), BF16),
         vmem((4, LAT, LANES), BF16),
-        vmem((8, 144, HD), BF16),
-        vmem((8, 144, HD), BF16),
+        vmem((8, SHARE, HD), BF16),
+        vmem((8, SHARE, HD), BF16),
+        vmem((WPACK, HD), BF16),
         vmem((3 * WID, HD), BF16),
         vmem((2, 2, 16, LAT, LANES), BF16),
         vmem((2, MCOLS, LANES), BF16),

time: 59.6 us -> 57.5 us (0.965)
  Pallas kernels: 58.8 us -> 56.8 us
    pallas_call x1, Pallas kernels: 57.1 us -> 55 us  [per_device(): pl.pallas_call(kernel, out_shape=(jax.ShapeDtypeStruct((LAT, ROWS), BF16)...]
where the time goes in v7:
time: 57.5 us; the launch traced here: 57.4 us
  Pallas kernels  56.8 us (99%)
  between operations  0.64 us (1%)
    pallas_call x1, Pallas kernels, per_device(): pl.pallas_call(kernel, out_shape=(jax.ShapeDtypeStruct((LAT, ROWS), BF16)...  55 us
    pallas_call x1, Pallas kernels, per_device(): pl.pallas_call(leave, out_shape=(jax.ShapeDtypeStruct((LAT, ROWS), BF16),...  1.72 us

profile of v7, /device:TPU:1, one launch (start us, length us, event | category | flops | bytes accessed | tf_op | source)
XLA Modules:
  0.0 57.4 jit_solution(881407880162016199)
XLA Ops:
  0.6 55.0 %shard_map.131 = (bf16[64,192]{1,0:T(8,128)(2,1)}, bf16[192,768]{1,0:T(8,128)(2,1)}) custom-call(bf16[192,3072]{1,0:T(8,128)(2,1)} %pixels.1, bf16[3072,512]{1,0:T(8,128)(2,1)} %w_encode.1, bf16[64,512]{1,0:T(8,128)(2,1)} %bitcast.9, s32[1,192]{1,0:T(1,128)} %bitcast.14, bf16[64,3072]{1,0:T(8,128)(2,1)} %w_embed.1, f32[1,3072]{1,0:T(1,128)} %bitcast.11, ...), custom_call_target="tpu_custom_call" | custom-call | tf_op jit(solution)/shard_map/pallas_call | solution.py:493
  55.7 1.7 %shard_map.132 = (bf16[64,192]{1,0:T(8,128)(2,1)}, bf16[192,768]{1,0:T(8,128)(2,1)}) custom-call(bf16[64,192]{1,0:T(8,128)(2,1)} %get-tuple-element.6.lat_ref, bf16[192,768]{1,0:T(8,128)(2,1)} %get-tuple-element.7.block_ref), custom_call_target="tpu_custom_call" | custom-call | tf_op jit(solution)/shard_map/pallas_call | solution.py:501

commit v8 on v7

--- a/solution.py
+++ b/solution.py
@@ -59,22 +59,22 @@
     b = z * 4 + y
     at = z * (x * 4 + y) + (1 - z) * (y * 4 + x)
     sibling = {"sec": s + 1 - 2 * c}
-    tp_peers = [{"tp": (t + k) % 4} for k in range(1, 4)]
+    tp_peers = [{"tp": (t + k) % 4} for k in (2, 1, 3)]
     x_at = [(x + k) % 4 for k in range(1, 4)]
     x_peers = [{"sec": s + (xx - x) * 8} for xx in x_at]
-    b_at = [(b + k) % 8 for k in range(1, 8)]
+    b_at = [(b + k) % 8 for k in (2, 6, 1, 3, 5, 7, 4)]
     b_peers = [{"sec": (bb // 4) * 32 + x * 8 + (bb % 4) * 2 + c} for bb in b_at]
     y_peers = [{"sec": s + ((y + k) % 4 - y) * 2} for k in range(1, 4)]
     cross_x = [{"sec": s + (1 - 2 * z) * 32 + (xx - x) * 8} for xx in x_at]
     inner = z * y + (1 - z) * x
     stride = 8 - 6 * z
-    plane_peers = [{"sec": s + ((inner + k) % 4 - inner) * stride} for k in range(1, 4)]
-    plane_peers += [
-        {"sec": s + (1 - 2 * z) * 32 + ((inner + k) % 4 - inner) * stride} for k in range(4)
+    plane_peers = [
+        {"sec": s + far * (1 - 2 * z) * 32 + ((inner + k) % 4 - inner) * stride}
+        for far, k in ((1, 2), (0, 2), (1, 1), (1, 3), (0, 1), (0, 3), (1, 0))
     ]
     m_peer = {"tp": s // 16, "sec": (t // 2) * 32 + (2 * (t % 2) + x % 2) * 8 + y * 2 + 1 - c}
     a = x * 2 + c
-    a_at = [(a + k) % 8 for k in range(1, 8)]
+    a_at = [(a + k) % 8 for k in (4, 5, 3, 2, 6, 1, 7)]
     a_peers = [{"sec": z * 32 + (aa // 2) * 8 + y * 2 + aa % 2} for aa in a_at]
 
     sent = []
@@ -97,13 +97,11 @@
     by_x = pl.ds(x * 4, 4)
 
     def spread_rest(ref):
-        pairs = []
-        for k in range(3):
-            pairs.append(
-                (
-                    push(ref.at[0, c, by_y], ref.at[0, c, by_y], y_peers[k]),
-                    push(ref.at[1, c, by_x], ref.at[1, c, by_x], x_peers[k]),
-                )
+        pairs = {}
+        for k in (1, 0, 2):
+            pairs[k] = (
+                push(ref.at[0, c, by_y], ref.at[0, c, by_y], y_peers[k]),
+                push(ref.at[1, c, by_x], ref.at[1, c, by_x], x_peers[k]),
             )
         return pairs
 

time: 57.5 us -> 56.8 us (0.988)
  Pallas kernels: 56.8 us -> 56.1 us
    pallas_call x1, Pallas kernels: 55 us -> 54.3 us  [per_device(): pl.pallas_call(kernel, out_shape=(jax.ShapeDtypeStruct((LAT, ROWS), BF16)...]
where the time goes in v8:
time: 56.8 us; the launch traced here: 56.7 us
  Pallas kernels  56.1 us (99%)
  between operations  0.64 us (1%)
    pallas_call x1, Pallas kernels, per_device(): pl.pallas_call(kernel, out_shape=(jax.ShapeDtypeStruct((LAT, ROWS), BF16)...  54.3 us
    pallas_call x1, Pallas kernels, per_device(): pl.pallas_call(leave, out_shape=(jax.ShapeDtypeStruct((LAT, ROWS), BF16),...  1.72 us

profile of v8, /device:TPU:1, one launch (start us, length us, event | category | flops | bytes accessed | tf_op | source)
XLA Modules:
  0.0 56.7 jit_solution(10309089402056623599)
XLA Ops:
  0.6 54.3 %shard_map.131 = (bf16[64,192]{1,0:T(8,128)(2,1)}, bf16[192,768]{1,0:T(8,128)(2,1)}) custom-call(bf16[192,3072]{1,0:T(8,128)(2,1)} %pixels.1, bf16[3072,512]{1,0:T(8,128)(2,1)} %w_encode.1, bf16[64,512]{1,0:T(8,128)(2,1)} %bitcast.9, s32[1,192]{1,0:T(1,128)} %bitcast.14, bf16[64,3072]{1,0:T(8,128)(2,1)} %w_embed.1, f32[1,3072]{1,0:T(1,128)} %bitcast.11, ...), custom_call_target="tpu_custom_call" | custom-call | tf_op jit(solution)/shard_map/pallas_call | solution.py:491
  55.0 1.7 %shard_map.132 = (bf16[64,192]{1,0:T(8,128)(2,1)}, bf16[192,768]{1,0:T(8,128)(2,1)}) custom-call(bf16[64,192]{1,0:T(8,128)(2,1)} %get-tuple-element.6.lat_ref, bf16[192,768]{1,0:T(8,128)(2,1)} %get-tuple-element.7.block_ref), custom_call_target="tpu_custom_call" | custom-call | tf_op jit(solution)/shard_map/pallas_call | solution.py:499

commit v9 on v8

--- a/solution.py
+++ b/solution.py
@@ -319,7 +319,7 @@
                 for copy in lat_rest[j - 1]:
                     copy.wait_recv()
                 lat_c.append(hand_over(slots, j))
-        if k == 1:
+        if k == 2:
             m_move.wait_recv()
             m_slots[z, c, at] = m_in[1]
             m_plane = spread_plane(m_slots)
@@ -378,16 +378,11 @@
         if h + 1 < HEADS:
             following = running[h + 1]
         for n in range(CHUNKS):
-            if h == 0 and n == 4:
+            if h == 0 and n == 10:
                 for copy in m_plane:
                     copy.wait_recv()
                 m_rest = spread_rest(m_slots)
                 m_c = list(hand_over(m_slots, 0))
-            if h == 2 and n == CHUNKS // 2:
-                for j in range(1, 4):
-                    for copy in m_rest[j - 1]:
-                        copy.wait_recv()
-                    m_c += hand_over(m_slots, j)
             if h + 1 < HEADS:
                 following = score(n, h + 1, following)
             added += weigh(n, h, most)
@@ -399,6 +394,10 @@
         packed[h, t] = jnp.where(lane_q[0 : ROWS // 2] < LAT, mixed[0 : ROWS // 2, :], lower).astype(BF16)
         o_heads.append([push(packed.at[h, t], packed.at[h, t], device) for device in tp_peers])
 
+    for j in range(1, 4):
+        for copy in m_rest[j - 1]:
+            copy.wait_recv()
+        m_c += hand_over(m_slots, j)
     for copy in m_c:
         copy.wait_recv()
     for slot in range(64):

time: 56.8 us -> 58.5 us (1.030)
  Pallas kernels: 56.1 us -> 57.8 us
    pallas_call x1, Pallas kernels: 54.3 us -> 56.1 us  [per_device(): pl.pallas_call(kernel, out_shape=(jax.ShapeDtypeStruct((LAT, ROWS), BF16)...]
where the time goes in v9:
time: 58.5 us; the launch traced here: 58.4 us
  Pallas kernels  57.8 us (99%)
  between operations  0.64 us (1%)
    pallas_call x1, Pallas kernels, per_device(): pl.pallas_call(kernel, out_shape=(jax.ShapeDtypeStruct((LAT, ROWS), BF16)...  56.1 us
    pallas_call x1, Pallas kernels, per_device(): pl.pallas_call(leave, out_shape=(jax.ShapeDtypeStruct((LAT, ROWS), BF16),...  1.72 us

profile of v9, /device:TPU:1, one launch (start us, length us, event | category | flops | bytes accessed | tf_op | source)
XLA Modules:
  0.0 58.4 jit_solution(16291209901110599901)
XLA Ops:
  0.6 56.1 %shard_map.131 = (bf16[64,192]{1,0:T(8,128)(2,1)}, bf16[192,768]{1,0:T(8,128)(2,1)}) custom-call(bf16[192,3072]{1,0:T(8,128)(2,1)} %pixels.1, bf16[3072,512]{1,0:T(8,128)(2,1)} %w_encode.1, bf16[64,512]{1,0:T(8,128)(2,1)} %bitcast.9, s32[1,192]{1,0:T(1,128)} %bitcast.14, bf16[64,3072]{1,0:T(8,128)(2,1)} %w_embed.1, f32[1,3072]{1,0:T(1,128)} %bitcast.11, ...), custom_call_target="tpu_custom_call" | custom-call | tf_op jit(solution)/shard_map/pallas_call | solution.py:490
  56.7 1.7 %shard_map.132 = (bf16[64,192]{1,0:T(8,128)(2,1)}, bf16[192,768]{1,0:T(8,128)(2,1)}) custom-call(bf16[64,192]{1,0:T(8,128)(2,1)} %get-tuple-element.6.lat_ref, bf16[192,768]{1,0:T(8,128)(2,1)} %get-tuple-element.7.block_ref), custom_call_target="tpu_custom_call" | custom-call | tf_op jit(solution)/shard_map/pallas_call | solution.py:498
